TPU v7x, 256 devices: a whole 4x4x8 slice. The times are simulated.
256 devices in a mesh: lines: 64 (over z, y, core), seg: 4 (over x).
Axes of the slice: x: 4, y: 4, z: 8, core: 2. Of those that a mesh axis runs over, the one named last changes fastest.
Arguments:
- diag_blocks: float32 [128, 16, 4096], P('lines', 'seg'), may hold values from -0.0021 to 0.0221, as said below
- couplings: float32 [128, 16, 4096], P('lines', 'seg'), may hold values from -0.363 to 1.363
- cross_weight: float32 [128, 1024], P('lines', 'seg'), may hold values from 0.001 to 0.0033
- right_side: float32 [128, 1024], P('lines', 'seg'), may hold values from -2.4 to 2.4
Outputs:
- solution_field: float32 [128, 1024], P('lines', 'seg')
- residual: float32 [128, 1024], P('lines', 'seg')
Inputs may be any that keep to these rules, and one draw needn't show every extreme that they name: Every block of diag_blocks is symmetric positive definite, every block of couplings is symmetric positive semidefinite, and the operator A is symmetric positive definite.
All inputs are finite; a program needn't handle non-finite values.
Results may differ from a plain program's by a relative error of at most 0.00065.
Values sent between devices are 32-bit elements; how exact they have to be, the bound alone decides.
A program may use at most 64 MiB of HBM per device.

v0:
```python
import jax
import jax.numpy as jnp
from jax import lax
from jax.sharding import PartitionSpec as P

BLOCK = 64
ITERS = 4


precise = lax.Precision.HIGHEST


def passed_along(array, axis, by):
    devices = lax.axis_size(axis)
    pairs = [(i, i + by) for i in range(devices) if 0 <= i + by < devices]
    return lax.ppermute(array, axis, pairs)


def from_behind(value, axis, steps):
    count = lax.axis_size(axis)
    pairs = [(source, (source + steps) % count) for source in range(count)]
    return lax.ppermute(value, axis, pairs)


def padded(array, sides, width, wrap):
    for axis, dim in sides:
        devices, length = (lax.axis_size(axis), array.shape[dim])
        up = [(i, (i + 1) % devices) for i in range(devices if wrap else devices - 1)]
        down = [(j, i) for i, j in up]
        last = lax.slice_in_dim(array, length - width, length, axis=dim)
        initial = lax.slice_in_dim(array, 0, width, axis=dim)
        before = lax.ppermute(last, axis, up)
        after = lax.ppermute(initial, axis, down)
        array = jnp.concatenate([before, array, after], axis=dim)
    return array


def matmul_plain(left, right):
    return jnp.einsum("lij,ljk->lik", left, right, precision=precise)


def matmul_left_t(left, right):
    return jnp.einsum("lji,ljk->lik", left, right, precision=precise)


def matmul_right_t(left, right):
    return jnp.einsum("lij,lkj->lik", left, right, precision=precise)


def matvec_plain(left, right):
    return jnp.einsum("lij,lj->li", left, right, precision=precise)


def matvec_left_t(left, right):
    return jnp.einsum("lji,lj->li", left, right, precision=precise)


def spd_inverse(matrix):
    lower_factor = jnp.linalg.cholesky(matrix)
    identity = jnp.broadcast_to(jnp.eye(matrix.shape[-1], dtype=matrix.dtype), matrix.shape)
    lower_inv = jax.scipy.linalg.solve_triangular(lower_factor, identity, lower=True)
    return jnp.einsum("...ki,...kj->...ij", lower_inv, lower_inv, precision=precise)


def block_factor(diag_seq, link_seq):
    zero_block = jnp.zeros_like(diag_seq[:1])
    link_before = jnp.concatenate([zero_block, link_seq], axis=0)
    link_after = jnp.concatenate([link_seq, zero_block], axis=0)

    def advance(carry_link, pieces):
        diag_now, before_now, after_now = pieces
        schur_block = diag_now - matmul_left_t(before_now, carry_link)
        inverse = spd_inverse(schur_block)
        coupled = matmul_plain(inverse, after_now)
        return (coupled, (inverse, coupled))

    last_coupled, outputs = lax.scan(advance, zero_block[0], (diag_seq, link_before, link_after))
    return outputs


def block_solve(inverses, coupled, rhs_seq):
    coupled_before = jnp.concatenate([jnp.zeros_like(coupled[:1]), coupled[:-1]], axis=0)

    def forward(prev_value, pieces):
        link_now, rhs_now = pieces
        current = rhs_now - jnp.einsum("lji,lj...->li...", link_now, prev_value, precision=precise)
        return (current, current)

    last_forward, reduced = lax.scan(forward, jnp.zeros_like(rhs_seq[0]), (coupled_before, rhs_seq))

    def backward(next_value, pieces):
        inverse, link_now, reduced_now = pieces
        current = jnp.einsum("lij,lj...->li...", inverse, reduced_now, precision=precise)
        current = current - jnp.einsum("lij,lj...->li...", link_now, next_value, precision=precise)
        return (current, current)

    last_backward, result = lax.scan(
        backward, jnp.zeros_like(rhs_seq[0]), (inverses, coupled, reduced), reverse=True
    )
    return result


def energy_total(residual, search):
    return lax.psum(jnp.sum(residual * search), ("lines", "seg"))


def local(diag_blocks, couplings, cross_weight, right_side):
    line_count, flat_width = right_side.shape
    elem_count = flat_width // BLOCK
    position = lax.axis_index("seg")
    seg_count = lax.axis_size("seg")

    def to_sequence(vector):
        return vector.reshape(line_count, elem_count, BLOCK).transpose(1, 0, 2)

    def from_sequence(sequence):
        return sequence.transpose(1, 0, 2).reshape(line_count, elem_count * BLOCK)

    mass_seq = diag_blocks.reshape(line_count, elem_count, BLOCK, BLOCK).transpose(1, 0, 2, 3)
    edge_seq = couplings.reshape(line_count, elem_count, BLOCK, BLOCK).transpose(1, 0, 2, 3)
    link_seq = -edge_seq
    keep_mask = jnp.where(position == seg_count - 1, 0.0, 1.0).astype(jnp.float32)
    link_out = link_seq[elem_count - 1] * keep_mask
    link_in = passed_along(link_out, "seg", 1)
    edge_prior = jnp.concatenate([-link_in[None], edge_seq[:-1]], axis=0)
    diag_seq = mass_seq + edge_seq + edge_prior
    weight_before = from_behind(cross_weight[line_count - 1 :], "lines", 1)
    weight_prev = jnp.concatenate([weight_before, cross_weight[:-1]], axis=0)
    link_used = jnp.concatenate([link_seq[: elem_count - 1], link_out[None]], axis=0)
    link_prior = jnp.concatenate([link_in[None], link_used[:-1]], axis=0)
    inner_inv, inner_link = block_factor(diag_seq[: elem_count - 1], link_seq[: elem_count - 2])
    link_last = link_seq[elem_count - 2]
    identity = jnp.broadcast_to(jnp.eye(BLOCK, dtype=diag_seq.dtype), (line_count, BLOCK, BLOCK))
    unit_rhs = (
        jnp.zeros((elem_count - 1, line_count, BLOCK, BLOCK), diag_seq.dtype).at[0].set(identity)
    )
    spikes = block_solve(inner_inv, inner_link, unit_rhs)
    first_first = spikes[0]
    last_first = spikes[elem_count - 2]
    last_last = inner_inv[elem_count - 2]
    own_block = diag_seq[elem_count - 1] - matmul_left_t(
        link_last, matmul_plain(last_last, link_last)
    )
    back_block = -matmul_right_t(matmul_plain(link_in, first_first), link_in)
    upper_block = -matmul_plain(matmul_right_t(link_in, last_first), link_last)
    back_next, upper_next = passed_along((back_block, upper_block), "seg", -1)
    sep_diag = own_block + back_next

    def eliminate(sweep_turn, received):
        inverse = spd_inverse(sep_diag - received)
        update = matmul_left_t(upper_next, matmul_plain(inverse, upper_next))
        return passed_along(update, "seg", 1)

    schur_received = lax.fori_loop(0, seg_count - 1, eliminate, jnp.zeros_like(sep_diag))
    sep_inverse = spd_inverse(sep_diag - schur_received)

    def precondition(vector):
        sequence = to_sequence(vector)
        inner_sol = block_solve(inner_inv, inner_link, sequence[: elem_count - 1])
        own_rhs = sequence[elem_count - 1] - matvec_left_t(link_last, inner_sol[elem_count - 2])
        back_rhs = -matvec_plain(link_in, inner_sol[0])
        sep_rhs = own_rhs + passed_along(back_rhs, "seg", -1)

        def forward_step(sweep_turn, received):
            eliminated = sep_rhs - received
            carried = matvec_left_t(upper_next, matvec_plain(sep_inverse, eliminated))
            return passed_along(carried, "seg", 1)

        forward_received = lax.fori_loop(0, seg_count - 1, forward_step, jnp.zeros_like(sep_rhs))
        eliminated = sep_rhs - forward_received

        def backward_step(sweep_turn, right_value):
            solved = matvec_plain(sep_inverse, eliminated - matvec_plain(upper_next, right_value))
            return passed_along(solved, "seg", -1)

        right_value = lax.fori_loop(0, seg_count - 1, backward_step, jnp.zeros_like(sep_rhs))
        sep_own = matvec_plain(sep_inverse, eliminated - matvec_plain(upper_next, right_value))
        sep_left = passed_along(sep_own, "seg", 1)
        corrected = sequence[: elem_count - 1]
        corrected = corrected.at[0].add(-matvec_left_t(link_in, sep_left))
        corrected = corrected.at[elem_count - 2].add(-matvec_plain(link_last, sep_own))
        inner_field = block_solve(inner_inv, inner_link, corrected)
        return from_sequence(jnp.concatenate([inner_field, sep_own[None]], axis=0))

    solution_field = jnp.zeros_like(right_side)
    residual = right_side
    search = precondition(residual)
    direction = search
    energy = energy_total(residual, search)
    for sweep_turn in range(ITERS):
        operate_sequence = to_sequence(direction)
        elem_sides = padded(direction, (("seg", 1),), BLOCK, False)
        before_edge = elem_sides[:, :BLOCK]
        after_edge = elem_sides[:, flat_width + BLOCK :]
        after_vals = jnp.concatenate([operate_sequence[1:], after_edge[None]], axis=0)
        before_vals = jnp.concatenate([before_edge[None], operate_sequence[:-1]], axis=0)
        line_part = jnp.einsum("elij,elj->eli", diag_seq, operate_sequence, precision=precise)
        line_part = line_part + jnp.einsum(
            "elij,elj->eli", link_used, after_vals, precision=precise
        )
        line_part = line_part + jnp.einsum(
            "elji,elj->eli", link_prior, before_vals, precision=precise
        )
        line_rows = padded(direction, (("lines", 0),), 1, True)
        across = cross_weight * line_rows[2:] + weight_prev * line_rows[:-2]
        image = from_sequence(line_part) - across
        curvature_sum = lax.psum(jnp.sum(direction * image), ("lines", "seg"))
        step_size = energy / curvature_sum
        solution_field = solution_field + step_size * direction
        residual = residual - step_size * image
        if sweep_turn + 1 < ITERS:
            search = precondition(residual)
            new_energy = energy_total(residual, search)
            direction = search + new_energy / energy * direction
            energy = new_energy
    return (solution_field, residual)


def solution(mesh):
    return jax.shard_map(
        local,
        mesh=mesh,
        in_specs=(
            P("lines", "seg", None),
            P("lines", "seg", None),
            P("lines", "seg"),
            P("lines", "seg"),
        ),
        out_specs=(P("lines", "seg"), P("lines", "seg")),
        check_vma=False,
    )
```

profile of v0, /device:TPU:1, one launch (start us, length us, event | category | flops | bytes accessed | tf_op | source)
XLA Modules:
  0.0 983.5 jit_solution(10895354621627367332)
XLA Ops:
  13.0 69.3 %while.383 = (s32[]{:T(128)}, f32[2,64,64]{2,1,0:T(8,128)S(1)}, f32[3,2,64,64]{3,2,1,0:T(8,128)S(1)}, f32[3,2,64,64]{3,2,1,0:T(8,128)S(1)}, f32[3,2,64,64]{2,3,1...) while((s32[]{:T(128)}, f32[2,64,64]{2,1,0:T(8,128)S(1)}, ...), condition=%wide.region_3.6_spmd, body=%wide.region_0.5_spmd.sunk | while | flops 25247872 | bytes 1133661 | solution.py:77
  13.4 11.7 %custom-call.38 = f32[2,64,64]{2,1,0:T(8,128)S(1)} custom-call(f32[2,64,64]{2,1,0:T(8,128)S(1)} %fusion.530), custom_call_target="Cholesky" | custom-call | tf_op jit(solution)/shard_map/while/body/eval_jaxpr/jit(cholesky)/cholesky | solution.py:59
  25.4 9.8 custom-call.39
  36.5 11.7 %custom-call.38 = f32[2,64,64]{2,1,0:T(8,128)S(1)} custom-call(f32[2,64,64]{2,1,0:T(8,128)S(1)} %fusion.530), custom_call_target="Cholesky" | custom-call | tf_op jit(solution)/shard_map/while/body/eval_jaxpr/jit(cholesky)/cholesky | solution.py:59
  48.5 9.8 custom-call.39
  59.6 11.7 %custom-call.38 = f32[2,64,64]{2,1,0:T(8,128)S(1)} custom-call(f32[2,64,64]{2,1,0:T(8,128)S(1)} %fusion.530), custom_call_target="Cholesky" | custom-call | tf_op jit(solution)/shard_map/while/body/eval_jaxpr/jit(cholesky)/cholesky | solution.py:59
  71.6 9.8 custom-call.39
  96.9 83.9 %while.384 = (s32[]{:T(128)}, f32[2,64,64]{1,2,0:T(8,128)S(1)}, f32[2,64,64]{1,2,0:T(8,128)S(1)}, f32[2,64,64]{2,1,0:T(8,128)S(1)}, s32[]{:T(128)}) while((s32[]{:T(128)}, f32[2,64,64]{1,2,0:T(8,128)S(1)}, f32[2,64,64]{1,2,0:T(8,128)S(1)}, f32[2,64,64]{2,1,0:T(8,128)S(1)}, s32[]{:T(128)}) %tuple.746), condition=%wide.region_9.12_spmd, body=%wide.region_8.11_spmd.sunk | while | flops 25247872 | bytes 869481 | solution.py:154
  97.1 11.7 %custom-call.40 = f32[2,64,64]{2,1,0:T(8,128)S(1)} custom-call(f32[2,64,64]{2,1,0:T(8,128)S(1)} %fusion.541), custom_call_target="Cholesky" | custom-call | tf_op jit(solution)/shard_map/while/body/eval_jaxpr/jit(cholesky)/cholesky | solution.py:59
  109.1 9.8 custom-call.41
  124.8 11.7 %custom-call.40 = f32[2,64,64]{2,1,0:T(8,128)S(1)} custom-call(f32[2,64,64]{2,1,0:T(8,128)S(1)} %fusion.541), custom_call_target="Cholesky" | custom-call | tf_op jit(solution)/shard_map/while/body/eval_jaxpr/jit(cholesky)/cholesky | solution.py:59
  136.8 9.8 custom-call.41
  152.9 11.7 %custom-call.40 = f32[2,64,64]{2,1,0:T(8,128)S(1)} custom-call(f32[2,64,64]{2,1,0:T(8,128)S(1)} %fusion.541), custom_call_target="Cholesky" | custom-call | tf_op jit(solution)/shard_map/while/body/eval_jaxpr/jit(cholesky)/cholesky | solution.py:59
  164.9 9.8 custom-call.41
  180.9 11.7 %custom-call.32 = f32[2,64,64]{2,1,0:T(8,128)S(1)} custom-call(f32[2,64,64]{2,1,0:T(8,128)S(1)} %fusion.161), custom_call_target="Cholesky" | custom-call | tf_op jit(solution)/shard_map/jit(cholesky)/cholesky | solution.py:59
  192.9 9.8 custom-call.33
  203.3 14.2 %while.385 = (s32[]{:T(128)}, f32[2,64]{1,0:T(2,128)S(1)}, f32[2,64]{1,0:T(2,128)S(1)}, f32[2,64,64]{2,1,0:T(8,128)S(1)}, f32[2,64,64]{2,1,0:T(8,128)S(1)}, /*index=5*/s32[]{:T(128)}) while((s32[]{:T(128)}, f32[2,64]{1,0:T(2,128)S(1)}, f32[2,64]{1,0:T(2,128)S(1)}, f32[2,64,64]{2,1,0:T(8,128)S(1)}, f32[2,64,64]{2,1,0:T(8,128)S(1)}, ...), condition=%wide.region_15.18_spmd, body=%wide.region_14.17_spmd.sunk | while | flops 196738 | bytes 71277 | solution.py:169
  217.6 14.7 %while.386 = (s32[]{:T(128)}, f32[2,64]{1,0:T(2,128)S(1)}, f32[2,64,64]{2,1,0:T(8,128)S(1)}, f32[2,64]{1,0:T(2,128)S(1)}, f32[2,64,64]{2,1,0:T(8,128)S(1)}, /*index=5*/s32[]{:T(128)}) while((s32[]{:T(128)}, f32[2,64]{1,0:T(2,128)S(1)}, f32[2,64,64]{2,1,0:T(8,128)S(1)}, f32[2,64]{1,0:T(2,128)S(1)}, f32[2,64,64]{2,1,0:T(8,128)S(1)}, ...), condition=%wide.region_17.20_spmd, body=%wide.region_16.19_spmd.sunk | while | flops 196738 | bytes 71277 | solution.py:176
  245.5 11.9 %collective-permute-start.16 = (f32[1,256]{1,0:T(1,128)S(1)}, f32[1,256]{1,0:T(1,128)S(1)}, u32[]{:S(2)}, u32[]{:S(2)}) collective-permute-start(f32[1,256]{1,0:T(1,128)S(1)} %slice.440), channel_id=1, source_target_pairs={{4,0},{8,4},{12,8},{16,12},{20,16},{24,20},{28,24},{32,28},{36,32}... | collective-permute-start | bytes 3080 | tf_op jit(solution)/shard_map/ppermute | solution.py:33
  260.5 80.0 %all-reduce.3 = (f32[]{:T(128)}, f32[]{:T(128)}) all-reduce(f32[]{:T(128)} %get-tuple-element.2246, f32[]{:T(128)} %get-tuple-element.2245), channel_id=1, replica_groups=mesh['lines'=64,'seg'=4] {'lines','seg'}, use_global_device_ids=true, to_apply=%region_23.26 | all-reduce | flops 2 | bytes 16 | tf_op jit(solution)/shard_map/psum | solution.py:104
  348.5 13.2 %while.387 = (s32[]{:T(128)}, f32[2,64]{1,0:T(2,128)S(1)}, f32[2,64]{1,0:T(2,128)S(1)}, f32[2,64,64]{2,1,0:T(8,128)S(1)}, f32[2,64,64]{2,1,0:T(8,128)S(1)}, /*index=5*/s32[]{:T(128)}) while((s32[]{:T(128)}, f32[2,64]{1,0:T(2,128)S(1)}, f32[2,64]{1,0:T(2,128)S(1)}, f32[2,64,64]{2,1,0:T(8,128)S(1)}, f32[2,64,64]{2,1,0:T(8,128)S(1)}, ...), condition=%wide.region_31.34_spmd, body=%wide.region_30.33_spmd.sunk | while | flops 196738 | bytes 71277 | solution.py:169
  361.8 14.6 %while.388 = (s32[]{:T(128)}, f32[2,64]{1,0:T(2,128)S(1)}, f32[2,64,64]{2,1,0:T(8,128)S(1)}, f32[2,64]{1,0:T(2,128)S(1)}, f32[2,64,64]{2,1,0:T(8,128)S(1)}, /*index=5*/s32[]{:T(128)}) while((s32[]{:T(128)}, f32[2,64]{1,0:T(2,128)S(1)}, f32[2,64,64]{2,1,0:T(8,128)S(1)}, f32[2,64]{1,0:T(2,128)S(1)}, f32[2,64,64]{2,1,0:T(8,128)S(1)}, ...), condition=%wide.region_33.36_spmd, body=%wide.region_32.35_spmd.sunk | while | flops 196738 | bytes 71277 | solution.py:176
  384.2 83.0 %psum.58 = f32[]{:T(128)} all-reduce(f32[]{:T(128)} %multiply_reduce_fusion.5), channel_id=1, replica_groups=mesh['lines'=64,'seg'=4] {'lines','seg'}, use_global_device_ids=true, to_apply=%region_39.42 | all-reduce | flops 1 | bytes 8 | tf_op jit(solution)/shard_map/psum | solution.py:104
  477.8 76.3 %psum.59 = f32[]{:T(128)} all-reduce(f32[]{:T(128)} %get-tuple-element.2585), channel_id=1, replica_groups=mesh['lines'=64,'seg'=4] {'lines','seg'}, use_global_device_ids=true, to_apply=%region_41.44 | all-reduce | flops 1 | bytes 8 | tf_op jit(solution)/shard_map/psum | solution.py:207
  562.3 12.9 %while.389 = (s32[]{:T(128)}, f32[2,64]{1,0:T(2,128)S(1)}, f32[2,64]{1,0:T(2,128)S(1)}, f32[2,64,64]{2,1,0:T(8,128)S(1)}, f32[2,64,64]{2,1,0:T(8,128)S(1)}, /*index=5*/s32[]{:T(128)}) while((s32[]{:T(128)}, f32[2,64]{1,0:T(2,128)S(1)}, f32[2,64]{1,0:T(2,128)S(1)}, f32[2,64,64]{2,1,0:T(8,128)S(1)}, f32[2,64,64]{2,1,0:T(8,128)S(1)}, ...), condition=%wide.region_47.50_spmd, body=%wide.region_46.49_spmd.sunk | while | flops 196738 | bytes 71277 | solution.py:169
  575.1 14.6 %while.390 = (s32[]{:T(128)}, f32[2,64]{1,0:T(2,128)S(1)}, f32[2,64,64]{2,1,0:T(8,128)S(1)}, f32[2,64]{1,0:T(2,128)S(1)}, f32[2,64,64]{2,1,0:T(8,128)S(1)}, /*index=5*/s32[]{:T(128)}) while((s32[]{:T(128)}, f32[2,64]{1,0:T(2,128)S(1)}, f32[2,64,64]{2,1,0:T(8,128)S(1)}, f32[2,64]{1,0:T(2,128)S(1)}, f32[2,64,64]{2,1,0:T(8,128)S(1)}, ...), condition=%wide.region_49.52_spmd, body=%wide.region_48.51_spmd.sunk | while | flops 196738 | bytes 71277 | solution.py:176
  597.5 83.3 %psum.60 = f32[]{:T(128)} all-reduce(f32[]{:T(128)} %multiply_reduce_fusion.3), channel_id=1, replica_groups=mesh['lines'=64,'seg'=4] {'lines','seg'}, use_global_device_ids=true, to_apply=%region_55.58 | all-reduce | flops 1 | bytes 8 | tf_op jit(solution)/shard_map/psum | solution.py:104
  691.6 76.2 %psum.61 = f32[]{:T(128)} all-reduce(f32[]{:T(128)} %get-tuple-element.2583), channel_id=1, replica_groups=mesh['lines'=64,'seg'=4] {'lines','seg'}, use_global_device_ids=true, to_apply=%region_57.60 | all-reduce | flops 1 | bytes 8 | tf_op jit(solution)/shard_map/psum | solution.py:207
  775.8 12.8 %while.391 = (s32[]{:T(128)}, f32[2,64]{1,0:T(2,128)S(1)}, f32[2,64]{1,0:T(2,128)S(1)}, f32[2,64,64]{2,1,0:T(8,128)S(1)}, f32[2,64,64]{2,1,0:T(8,128)S(1)}, /*index=5*/s32[]{:T(128)}) while((s32[]{:T(128)}, f32[2,64]{1,0:T(2,128)S(1)}, f32[2,64]{1,0:T(2,128)S(1)}, f32[2,64,64]{2,1,0:T(8,128)S(1)}, f32[2,64,64]{2,1,0:T(8,128)S(1)}, ...), condition=%wide.region_63.66_spmd, body=%wide.region_62.65_spmd.sunk | while | flops 196738 | bytes 71277 | solution.py:169
  788.6 14.6 %while.392 = (s32[]{:T(128)}, f32[2,64]{1,0:T(2,128)S(1)}, f32[2,64,64]{2,1,0:T(8,128)S(1)}, f32[2,64]{1,0:T(2,128)S(1)}, f32[2,64,64]{2,1,0:T(8,128)S(1)}, /*index=5*/s32[]{:T(128)}) while((s32[]{:T(128)}, f32[2,64]{1,0:T(2,128)S(1)}, f32[2,64,64]{2,1,0:T(8,128)S(1)}, f32[2,64]{1,0:T(2,128)S(1)}, f32[2,64,64]{2,1,0:T(8,128)S(1)}, ...), condition=%wide.region_65.68_spmd, body=%wide.region_64.67_spmd.sunk | while | flops 196738 | bytes 71277 | solution.py:176
  810.9 83.1 %psum.62 = f32[]{:T(128)} all-reduce(f32[]{:T(128)} %multiply_reduce_fusion.1), channel_id=1, replica_groups=mesh['lines'=64,'seg'=4] {'lines','seg'}, use_global_device_ids=true, to_apply=%region_71.74 | all-reduce | flops 1 | bytes 8 | tf_op jit(solution)/shard_map/psum | solution.py:104
  904.8 76.3 %psum.63 = f32[]{:T(128)} all-reduce(f32[]{:T(128)} %get-tuple-element.2581), channel_id=1, replica_groups=mesh['lines'=64,'seg'=4] {'lines','seg'}, use_global_device_ids=true, to_apply=%region_73.76 | all-reduce | flops 1 | bytes 8 | tf_op jit(solution)/shard_map/psum | solution.py:207
  (755 shorter events, 268.8 us)
Async XLA Ops:
  1.9 9.4 collective-permute-start.9
  6.0 253.6 %collective-permute-start.17 = (f32[1,256]{1,0:T(1,128)S(1)}, f32[1,256]{1,0:T(1,128)S(1)}, u32[]{:S(2)}, u32[]{:S(2)}) collective-permute-start(f32[1,256]{1,0:T(1,128)S(1)} %get-tuple-element.2628), channel_id=1, source_target_pairs={{0,4},{4,8},{8,12},{12,16},{16,20},{20,24},{24,28},{28,32},{32,36}... | collective-permute-start | bytes 3080 | tf_op jit(solution)/shard_map/ppermute | solution.py:22
  85.6 11.1 %collective-permute-start.10 = (f32[2,64,64]{1,2,0:T(8,128)S(1)}, f32[2,64,64]{1,2,0:T(8,128)S(1)}, u32[]{:S(2)}, u32[]{:S(2)}) collective-permute-start(f32[2,64,64]{1,2,0:T(8,128)S(1)} %convolution_negate_fusion.1), channel_id=1, source_target_pairs={{1,0},{2,1},{3,2},{5,4},{6,5},{7,6},{9,8},{10,9},{11,10},{13,12},{... | collective-permute-start | bytes 98312 | tf_op jit(solution)/shard_map/ppermute | solution.py:16
  87.4 9.5 collective-permute-start.11
  91.1 5.6 collective-permute-start.12
  120.0 4.7 collective-permute-start
  147.7 5.0 collective-permute-start
  175.8 5.0 collective-permute-start
  203.7 4.4 collective-permute-start.1
  208.5 4.3 collective-permute-start.1
  218.0 4.6 collective-permute-start.2
  223.0 4.5 collective-permute-start.2
  227.9 4.3 collective-permute-start.2
  239.6 19.1 %collective-permute-start.14 = (f32[2,64]{1,0:T(2,128)S(1)}, f32[2,64]{1,0:T(2,128)S(1)}, u32[]{:S(2)}, u32[]{:S(2)}) collective-permute-start(f32[2,64]{1,0:T(2,128)S(1)} %get-tuple-element.2630), channel_id=1, source_target_pairs={{1,0},{2,1},{3,2},{5,4},{6,5},{7,6},{9,8},{10,9},{11,10},{13,12},{... | collective-permute-start | bytes 1544 | tf_op jit(solution)/shard_map/ppermute | solution.py:33
  241.2 17.5 %collective-permute-start.15 = (f32[2,64]{1,0:T(2,128)S(1)}, f32[2,64]{1,0:T(2,128)S(1)}, u32[]{:S(2)}, u32[]{:S(2)}) collective-permute-start(f32[2,64]{1,0:T(2,128)S(1)} %get-tuple-element.2631), channel_id=1, source_target_pairs={{0,1},{1,2},{2,3},{4,5},{5,6},{6,7},{8,9},{9,10},{10,11},{12,13},{... | collective-permute-start | bytes 1544 | tf_op jit(solution)/shard_map/ppermute | solution.py:32
  245.5 14.3 %collective-permute-start.16 = (f32[1,256]{1,0:T(1,128)S(1)}, f32[1,256]{1,0:T(1,128)S(1)}, u32[]{:S(2)}, u32[]{:S(2)}) collective-permute-start(f32[1,256]{1,0:T(1,128)S(1)} %slice.440), channel_id=1, source_target_pairs={{4,0},{8,4},{12,8},{16,12},{20,16},{24,20},{28,24},{32,28},{36,32}... | collective-permute-start | bytes 3080 | tf_op jit(solution)/shard_map/ppermute | solution.py:33
  362.2 4.6 collective-permute-start.4
  367.2 4.5 collective-permute-start.4
  372.1 4.3 collective-permute-start.4
  468.5 7.4 collective-permute-start.21
  469.8 6.1 collective-permute-start.22
  570.8 4.3 collective-permute-start.5
  575.6 4.6 collective-permute-start.6
  580.6 4.4 collective-permute-start.6
  585.4 4.3 collective-permute-start.6
  682.2 7.4 collective-permute-start.27
  683.9 6.1 collective-permute-start.28
  789.1 4.6 collective-permute-start.8
  794.1 4.4 collective-permute-start.8
  798.9 4.3 collective-permute-start.8
  895.4 7.4 collective-permute-start.33
  897.1 6.1 collective-permute-start.34
  (33 other events, 102.1 us)
where the time goes:
time: 986 us; the launch traced here: 984 us
  blocking collectives  558 us (57%)
  other arithmetic  160 us (16%)
  starting transfers between devices  134 us (14%)
  waiting for transfers between devices  65.7 us (7%)
  matrix products  44.5 us (5%)
  between operations  11 us (1%)
    psum x4, blocking collectives, energy_total(): return lax.psum(jnp.sum(residual * search), ('lines', 'seg'))  329 us
    psum x3, blocking collectives, local(): curvature_sum = lax.psum(jnp.sum(direction * image), ('lines', 'seg'))  229 us
    ppermute x38, starting transfers between devices, passed_along(): return lax.ppermute(array, axis, pairs)  91.8 us
    another operation x28, other arithmetic, spd_inverse(): lower_factor = jnp.linalg.cholesky(matrix)  83.2 us
    another operation x21, other arithmetic, spd_inverse(): jax.scipy.linalg.solve_triangular(lower_factor, identity, lower=True)  69.4 us
    ppermute x38, waiting for transfers between devices, passed_along(): return lax.ppermute(array, axis, pairs)  64.5 us
    ppermute x8, starting transfers between devices, padded(): after = lax.ppermute(initial, axis, down)  21.8 us
  transfers between devices with their start and end apart: 55, of which 39 were waited for; matrix products, arithmetic and copies ran while one was open for 18% of the time, Pallas kernels for 0%

commit v1 on v0

v1 whole, which is shorter than its diff:
```python
import functools

import jax
import jax.numpy as jnp
from jax import lax
from jax.experimental import pallas as pl
from jax.experimental.pallas import tpu as pltpu
from jax.sharding import PartitionSpec as P

B = 64
F32 = jnp.float32
MESH = pl.DeviceIdType.MESH
VMEM = pl.BlockSpec(memory_space=pltpu.VMEM)
EXACT = lax.Precision.HIGHEST


def mm(a, b):
    return jnp.dot(a, b, precision=EXACT, preferred_element_type=F32)


def mm_nt(a, b):
    return lax.dot_general(a, b, (((1,), (1,)), ((), ())), precision=EXACT, preferred_element_type=F32)


def invert(work, packs):
    lane = lax.broadcasted_iota(jnp.int32, (8, 2 * B), 1)
    half = jnp.where(lane < B, 0, B)
    inner = lane - half

    def step(i, carry):
        k = 2 * i
        at0, at1 = half + k, half + k + 1
        is0, is1 = inner == k, inner == k + 1
        both = jnp.logical_or(is0, is1)
        for p in range(packs):
            r0 = jnp.broadcast_to(work[pl.ds(B * p + k, 1), :], (8, 2 * B))
            r1 = jnp.broadcast_to(work[pl.ds(B * p + k + 1, 1), :], (8, 2 * B))
            a = jnp.take_along_axis(r0, at0, axis=1, mode="promise_in_bounds")
            b = jnp.take_along_axis(r0, at1, axis=1, mode="promise_in_bounds")
            d = jnp.take_along_axis(r1, at1, axis=1, mode="promise_in_bounds")
            inv = 1.0 / (a * d - b * b)
            ai, bi, di = a * inv, b * inv, d * inv
            n0 = jnp.where(is0, di, jnp.where(is1, -bi, di * r0 - bi * r1))
            n1 = jnp.where(is0, -bi, jnp.where(is1, ai, ai * r1 - bi * r0))
            for t in range(B // 8):
                rows = pl.ds(B * p + 8 * t, 8)
                tile = work[rows, :]
                c0 = jnp.take_along_axis(tile, at0, axis=1, mode="promise_in_bounds")
                c1 = jnp.take_along_axis(tile, at1, axis=1, mode="promise_in_bounds")
                work[rows, :] = jnp.where(both, 0.0, tile) - c0 * n0 - c1 * n1
            work[pl.ds(B * p + k, 1), :] = n0[:1]
            work[pl.ds(B * p + k + 1, 1), :] = n1[:1]
        return carry

    lax.fori_loop(0, B // 2, step, 0)


def interior_kernel(diag, coup, gz, hh, xyz, dmat, pmat, work):
    lines = diag.shape[0]
    last = lax.axis_index("seg") == lax.axis_size("seg") - 1
    not_first = lax.broadcasted_iota(jnp.int32, (4, 2 * B), 0) > 0
    for l in range(lines):
        for k in range(B * B // (2 * B)):
            cols = pl.ds(2 * B * k, 2 * B)
            edge = coup[l, :, cols]
            before = jnp.concatenate([edge[3:], edge[:3]], axis=0)
            full = diag[l, :, cols] + edge + jnp.where(not_first, before, 0.0)
            for dst, tile in ((dmat, full), (pmat, edge)):
                dst[pl.ds(4 * B * l + 2 * k, 4, stride=B), :] = tile
                dst[pl.ds(4 * B * l + 2 * k + 1, 4, stride=B), :] = jnp.concatenate([tile[:, B:], tile[:, :B]], axis=1)

    def d_of(l, e):
        return dmat[pl.ds(4 * B * l + B * e, B), :B]

    def p_of(l, e):
        return pmat[pl.ds(4 * B * l + B * e, B), :B]

    for l in range(lines):
        work[pl.ds(B * l, B), :] = jnp.concatenate([d_of(l, 1), d_of(l, 3)], axis=1)
    invert(work, lines)
    i1 = [work[pl.ds(B * l, B), :B] for l in range(lines)]
    i3 = [work[pl.ds(B * l, B), B:] for l in range(lines)]
    u1 = [mm(i1[l], p_of(l, 1)) for l in range(lines)]
    u3 = [mm(i3[l], p_of(l, 2)) for l in range(lines)]
    s2 = [d_of(l, 2) - mm(p_of(l, 1), u1[l]) - mm(p_of(l, 2), u3[l]) for l in range(lines)]
    work[pl.ds(0, B), :] = jnp.concatenate(s2, axis=1)
    invert(work, 1)
    eye = (
        lax.broadcasted_iota(jnp.int32, (B, 2 * B), 0) == lax.broadcasted_iota(jnp.int32, (B, 2 * B), 1)
    ).astype(F32)
    zero = jnp.zeros((B, B), F32)
    for l in range(lines):
        i2 = work[pl.ds(0, B), B * l : B * l + B]
        w1, w3 = mm(u1[l], i2), mm(u3[l], i2)
        g21, g23 = mm_nt(i2, u1[l]), mm_nt(i2, u3[l])
        g11, g13 = i1[l] + mm_nt(w1, u1[l]), mm_nt(w1, u3[l])
        g31, g33 = mm_nt(w3, u1[l]), i3[l] + mm_nt(w3, u3[l])
        gz[l, 0:B, :] = jnp.zeros((B, 4 * B), F32)
        gz[l, B : 2 * B, :] = jnp.concatenate([zero, g11, w1, g13], axis=1)
        gz[l, 2 * B : 3 * B, :] = jnp.concatenate([zero, g21, i2, g23], axis=1)
        gz[l, 3 * B :, :] = jnp.concatenate([zero, g31, w3, g33], axis=1)
        p0 = p_of(l, 0)
        p3 = jnp.where(last, 0.0, p_of(l, 3))
        h1 = mm(jnp.concatenate([g11, g21, g31], axis=0), p0)
        h3 = mm(jnp.concatenate([g13, g23, g33], axis=0), p3)
        hh[l, 0:B, :] = eye
        hh[l, B:, :] = jnp.concatenate([h1, h3], axis=1)
        x = d_of(l, 0) - mm(p0, h1[:B])
        y = p3 - mm(p3, h3[2 * B :])
        xyz[l, :, :] = jnp.concatenate([x, y], axis=1)
        xyz[lines, :, B * l : B * l + B] = mm(p0, h3[:B])


def meet(peers):
    barrier = pltpu.get_barrier_semaphore()
    for peer in peers:
        pl.semaphore_signal(barrier, inc=1, device_id=peer, device_id_type=MESH)
    pl.semaphore_wait(barrier, len(peers))


def gather_kernel(mine, out, slots, send_sem, recv_sem):
    line, me = lax.axis_index("lines"), lax.axis_index("seg")
    count = slots.shape[0]
    others = [lax.rem(me + d, count) for d in range(1, count)]
    meet([(line, other) for other in others])
    sends = []
    for d, other in enumerate(others):
        copy = pltpu.make_async_remote_copy(
            src_ref=mine,
            dst_ref=slots.at[me],
            send_sem=send_sem.at[d],
            recv_sem=recv_sem.at[me],
            device_id=(line, other),
            device_id_type=MESH,
        )
        copy.start()
        sends.append(copy)
    out[me] = mine[...]
    for d, other in enumerate(others):
        pltpu.make_async_remote_copy(
            src_ref=mine,
            dst_ref=slots.at[other],
            send_sem=send_sem.at[d],
            recv_sem=recv_sem.at[other],
            device_id=(line, other),
            device_id_type=MESH,
        ).wait_recv()
        out[other] = slots[other]
    for copy in sends:
        copy.wait_send()


def reduced_kernel(xyz, hh, post, work, sigma):
    lines = hh.shape[0]
    me = lax.axis_index("seg")

    def diag_of(l, s):
        block = xyz[s, l, :, :B]
        return block if s == 0 else block + xyz[s - 1, l, :, B:]

    def z_of(l, s):
        return xyz[s, lines, :, B * l : B * l + B]

    for l in range(lines):
        work[pl.ds(B * l, B), :] = jnp.concatenate([diag_of(l, 0), diag_of(l, 3)], axis=1)
    invert(work, lines)
    every = range(lines)
    j0 = [work[pl.ds(B * l, B), :B] for l in every]
    j3 = [work[pl.ds(B * l, B), B:] for l in every]
    v0 = [mm(j0[l], z_of(l, 0)) for l in every]
    v3 = [mm_nt(j3[l], z_of(l, 2)) for l in every]
    s11 = [diag_of(l, 1) - mm(z_of(l, 0).T, v0[l]) for l in every]
    s22 = [diag_of(l, 2) - mm(z_of(l, 2), v3[l]) for l in every]
    work[pl.ds(0, B), :] = jnp.concatenate(s11, axis=1)
    invert(work, 1)
    j1 = [work[pl.ds(0, B), B * l : B * l + B] for l in every]
    v1 = [mm(j1[l], z_of(l, 1)) for l in every]
    s22 = [s22[l] - mm(z_of(l, 1).T, v1[l]) for l in every]
    work[pl.ds(0, B), :] = jnp.concatenate(s22, axis=1)
    invert(work, 1)
    for l in every:
        e22 = work[pl.ds(0, B), B * l : B * l + B]
        e12, e21 = mm(v1[l], e22), mm_nt(e22, v1[l])
        e11 = j1[l] + mm_nt(e12, v1[l])
        e01, e02 = mm(v0[l], e11), mm(v0[l], e12)
        e10, e20 = mm_nt(e11, v0[l]), mm_nt(e21, v0[l])
        e31, e32 = mm(v3[l], e21), mm(v3[l], e22)
        e13, e23 = mm_nt(e12, v3[l]), mm_nt(e22, v3[l])
        e00 = j0[l] + mm_nt(e01, v0[l])
        e33 = j3[l] + mm_nt(e32, v3[l])
        e03, e30 = mm_nt(e02, v3[l]), mm(v3[l], e20)
        for s, row in enumerate(((e00, e01, e02, e03), (e10, e11, e12, e13), (e20, e21, e22, e23), (e30, e31, e32, e33))):
            sigma[pl.ds(B * s, B), :] = jnp.concatenate(row, axis=1)
        sigma[pl.ds(4 * B, B), :] = jnp.zeros((B, 4 * B), F32)
        rows = sigma[pl.ds(pl.multiple_of(B * me, B), 2 * B), :]
        post[l] = mm(hh[l], rows).T


def solve_kernel(
    dims, gz, hh, post, weight, right, out_x, out_r,
    edge, edge_in, sep, sep_in, sums, sums_in, edge_send, edge_recv, sep_send, sep_recv, sum_send, sum_recv,
):
    nl, ns, ny = dims
    line, me = lax.axis_index("lines"), lax.axis_index("seg")
    left, right_of = lax.rem(line + nl - 1, nl), lax.rem(line + 1, nl)
    core, y_at, z_at = lax.rem(line, 2), lax.rem(line // 2, ny), line // (2 * ny)
    nz = nl // (2 * ny)

    def near(index):
        return ((z_at * ny + index // ns) * 2 + core, lax.rem(index, ns))

    def far(index):
        return (((index // 2) * ny + y_at) * 2 + lax.rem(index, 2), me)

    groups = ((near, ns * ny, y_at * ns + me), (far, 2 * nz, z_at * 2 + core))
    peers = [(left, me), (right_of, me)] + [(line, lax.rem(me + d, ns)) for d in range(1, ns)]
    for place, size, own in groups:
        peers += [place(lax.rem(own + d, size)) for d in range(1, size)]
    meet(peers)
    sends = []

    def edges(turn, low, high):
        copies = []
        for side, (row, to) in enumerate(((low, left), (high, right_of))):
            edge[turn, side] = row
            copy = pltpu.make_async_remote_copy(
                src_ref=edge.at[turn, side],
                dst_ref=edge_in.at[turn, side],
                send_sem=edge_send.at[turn, side],
                recv_sem=edge_recv.at[turn, side],
                device_id=(to, me),
                device_id_type=MESH,
            )
            copy.start()
            copies.append(copy)
            sends.append(copy)
        for copy in copies:
            copy.wait_recv()
        return edge_in[turn, 1], edge_in[turn, 0]

    def spread(buffer, inbox, send_sem, recv_sem, own, size, place):
        for d in range(1, size):
            copy = pltpu.make_async_remote_copy(
                src_ref=buffer,
                dst_ref=inbox.at[own],
                send_sem=send_sem.at[d],
                recv_sem=recv_sem.at[own],
                device_id=place(lax.rem(own + d, size)),
                device_id_type=MESH,
            )
            copy.start()
            sends.append(copy)
        inbox[own] = buffer[...]
        for d in range(1, size):
            other = lax.rem(own + d, size)
            pltpu.make_async_remote_copy(
                src_ref=buffer,
                dst_ref=inbox.at[other],
                send_sem=send_sem.at[d],
                recv_sem=recv_sem.at[other],
                device_id=place(other),
                device_id_type=MESH,
            ).wait_recv()

    low_lane = lax.broadcasted_iota(jnp.int32, (1, 2 * B), 1) < B

    def swap(row):
        return jnp.concatenate([row[:, B:], row[:, :B]], axis=1)

    def precondition(turn, t):
        z = []
        for l in range(2):
            lhs = jnp.broadcast_to(t[l], (8, 4 * B))
            z.append(mm(lhs, gz[l])[:1])
            sep[turn, pl.ds(l, 1), :] = mm(lhs, hh[l])[:1]
        spread(
            sep.at[turn], sep_in.at[turn], sep_send.at[turn], sep_recv.at[turn], me, ns, lambda s: (line, s)
        )
        out = []
        for l in range(2):
            g0, g1, g2, g3 = (sep_in[turn, s, pl.ds(l, 1), :] for s in range(4))
            f01 = jnp.where(low_lane, g0, g0 + swap(g1))
            f23 = g2 + jnp.where(low_lane, swap(g1), swap(g3))
            f = jnp.broadcast_to(jnp.concatenate([f01, f23], axis=1), (8, 4 * B))
            out.append(z[l] + mm(f, post[l])[:1])
        return out

    w = [weight[pl.ds(0, 1), :], weight[pl.ds(1, 1), :]]
    before_w, _ = edges(4, w[0], w[1])

    def across(turn, y):
        before, after = edges(turn, y[0], y[1])
        return [w[0] * y[1] + before_w * before, w[1] * after + w[0] * y[0]]

    ts = [[right[pl.ds(0, 1), :], right[pl.ds(1, 1), :]]]
    ys = []
    for turn in range(4):
        ys.append(precondition(turn, ts[turn]))
        ts.append(across(turn, ys[turn]))
    for i in range(8):
        y, t = ys[i // 2], ts[(i + 1) // 2]
        both = y[0] * t[0] + y[1] * t[1]
        sums[0, pl.ds(i, 1), :] = both[:, : 2 * B] + both[:, 2 * B :]
    for stage, (place, size, own) in enumerate(groups):
        spread(
            sums.at[stage], sums_in.at[stage], sum_send.at[stage], sum_recv.at[stage], own, size, place
        )
        total = sums_in[stage, 0]
        for i in range(1, size):
            total = total + sums_in[stage, i]
        sums[stage + 1] = total
    total = jnp.sum(total, axis=1, keepdims=True)
    g = [total[i : i + 1] for i in range(8)]
    m = [[g[i + j] for j in range(4)] + [-g[i + 4]] for i in range(4)]
    for k in range(3):
        inverse = 1.0 / m[k][k]
        for i in range(k + 1, 4):
            ratio = m[i][k] * inverse
            for j in range(k + 1, 5):
                m[i][j] = m[i][j] - ratio * m[k][j]
    d = [None] * 4 + [jnp.ones((1, 1), F32)]
    for k in (3, 2, 1, 0):
        value = m[k][4]
        for j in range(k + 1, 4):
            value = value - m[k][j] * d[j]
        d[k] = value / m[k][k]
    scale = 1.0 / (d[0] + d[1] + d[2] + d[3] + d[4])
    d = [value * scale for value in d]
    c = [None, None, None, d[4]]
    for k in (2, 1, 0):
        c[k] = c[k + 1] + d[k + 1]
    for l in range(2):
        x = c[0] * ys[0][l]
        r = d[0] * ts[0][l]
        for k in range(1, 4):
            x = x + c[k] * ys[k][l]
            r = r + d[k] * ts[k][l]
        out_x[pl.ds(l, 1), :] = x
        out_r[pl.ds(l, 1), :] = r + d[4] * ts[4][l]
    for copy in sends:
        copy.wait_send()


def local(diag_blocks, couplings, cross_weight, right_side):
    lines = right_side.shape[0]
    nl, ns = lax.axis_size("lines"), lax.axis_size("seg")
    ny = min(4, nl // 2)
    size = max(ns * ny, nl // ny)
    shape = jax.ShapeDtypeStruct
    gz, hh, xyz = pl.pallas_call(
        interior_kernel,
        out_shape=(
            shape((lines, 4 * B, 4 * B), F32),
            shape((lines, 4 * B, 2 * B), F32),
            shape((lines + 1, B, 2 * B), F32),
        ),
        in_specs=[VMEM] * 2,
        out_specs=[VMEM] * 3,
        scratch_shapes=[
            pltpu.VMEM((4 * B * lines, 2 * B), F32),
            pltpu.VMEM((4 * B * lines, 2 * B), F32),
            pltpu.VMEM((B * lines, 2 * B), F32),
        ],
        name="interior",
    )(diag_blocks, couplings)
    gathered = pl.pallas_call(
        gather_kernel,
        out_shape=shape((ns, lines + 1, B, 2 * B), F32),
        in_specs=[VMEM],
        out_specs=VMEM,
        scratch_shapes=[
            pltpu.VMEM((ns, lines + 1, B, 2 * B), F32),
            pltpu.SemaphoreType.DMA((ns - 1,)),
            pltpu.SemaphoreType.DMA((ns,)),
        ],
        compiler_params=pltpu.CompilerParams(collective_id=0, has_side_effects=True),
        name="gather",
    )(xyz)
    post = pl.pallas_call(
        reduced_kernel,
        out_shape=shape((lines, 4 * B, 4 * B), F32),
        in_specs=[VMEM] * 2,
        out_specs=VMEM,
        scratch_shapes=[
            pltpu.VMEM((B * lines, 2 * B), F32),
            pltpu.VMEM((5 * B, 4 * B), F32),
        ],
        name="reduced",
    )(gathered, hh)
    return pl.pallas_call(
        functools.partial(solve_kernel, (nl, ns, ny)),
        out_shape=(shape(right_side.shape, F32), shape(right_side.shape, F32)),
        in_specs=[VMEM] * 5,
        out_specs=[VMEM] * 2,
        scratch_shapes=[
            pltpu.VMEM((5, 2, 1, 4 * B), F32),
            pltpu.VMEM((5, 2, 1, 4 * B), F32),
            pltpu.VMEM((4, 8, 2 * B), F32),
            pltpu.VMEM((4, ns, 8, 2 * B), F32),
            pltpu.VMEM((3, 8, 2 * B), F32),
            pltpu.VMEM((2, size, 8, 2 * B), F32),
            pltpu.SemaphoreType.DMA((5, 2)),
            pltpu.SemaphoreType.DMA((5, 2)),
            pltpu.SemaphoreType.DMA((4, ns)),
            pltpu.SemaphoreType.DMA((4, ns)),
            pltpu.SemaphoreType.DMA((2, size)),
            pltpu.SemaphoreType.DMA((2, size)),
        ],
        compiler_params=pltpu.CompilerParams(collective_id=1, has_side_effects=True),
        name="solve",
    )(gz, hh, post, cross_weight, right_side)


def solution(mesh):
    return jax.shard_map(
        local,
        mesh=mesh,
        in_specs=(
            P("lines", "seg", None),
            P("lines", "seg", None),
            P("lines", "seg"),
            P("lines", "seg"),
        ),
        out_specs=(P("lines", "seg"), P("lines", "seg")),
        check_vma=False,
    )
```

time: 986 us -> 104 us (0.11)
  blocking collectives: 558 us -> 0 us
  other arithmetic: 160 us -> 0 us
  starting transfers between devices: 134 us -> 0 us
  Pallas kernels: 0 us -> 101 us
  waiting for transfers between devices: 65.7 us -> 0 us
  matrix products: 44.5 us -> 0 us
  between operations: 11 us -> 0.66 us
    psum x7 -> x0, blocking collectives: 558 us -> none  [the longest x4 329 us: energy_total(): return lax.psum(jnp.sum(residual * search), ('lines', 'seg'))]
    another operation x50 -> x0, other arithmetic: 153 us -> none  [the longest x28 83.2 us: spd_inverse(): lower_factor = jnp.linalg.cholesky(matrix)]
    ppermute x55 -> x0, starting transfers between devices: 134 us -> none  [the longest x38 91.8 us: passed_along(): return lax.ppermute(array, axis, pairs)]
    pallas_call x0 -> x4, Pallas kernels: none -> 101 us  [the longest x1 57 us: local(): pl.pallas_call(functools.partial(solve_kernel, (nl, ns, ny)), out_shape=(...]
    ppermute x55 -> x0, waiting for transfers between devices: 65.7 us -> none  [the longest x38 64.5 us: passed_along(): return lax.ppermute(array, axis, pairs)]
    dot_general x190 -> x0, matrix products: 42.4 us -> none  [the longest x52 10.3 us: matvec_plain(): return jnp.einsum('lij,lj->li', left, right, precision=precise)]
  transfers between devices with their start and end apart: 55 -> 0, of which waited for: 39 -> 0; matrix products, arithmetic and copies ran while one was open for 18% -> 0% of each run, Pallas kernels for 0% -> 0%
where the time goes in v1:
time: 104 us
  Pallas kernels  101 us (97%)
  local copies, waits for them, and re-layouts  1.93 us (2%)
    pallas_call x1, Pallas kernels, local(): pl.pallas_call(functools.partial(solve_kernel, (nl, ns, ny)), out_shape=(...  57 us
    pallas_call x1, Pallas kernels, local(): pl.pallas_call(reduced_kernel, out_shape=shape((lines, 4 * B, 4 * B), F32...  19.5 us
    pallas_call x1, Pallas kernels, local(): pl.pallas_call(interior_kernel, out_shape=(shape((lines, 4 * B, 4 * B), F...  14.6 us
    pallas_call x1, Pallas kernels, local(): pl.pallas_call(gather_kernel, out_shape=shape((ns, lines + 1, B, 2 * B),...  9.85 us

profile of v1, /device:TPU:1, one launch (start us, length us, event | category | flops | bytes accessed | tf_op | source)
XLA Modules:
  0.0 103.6 jit_solution(1679116532640365522)
XLA Ops:
  0.6 14.6 %interior.1 = (f32[2,256,256]{2,1,0:T(8,128)}, f32[2,256,128]{2,1,0:T(8,128)}, f32[3,64,128]{2,1,0:T(8,128)}) custom-call(f32[2,4,4096]{2,1,0:T(4,128)} %diag.1, f32[2,4,4096]{2,1,0:T(4,128)} %coup.1), custom_call_target="tpu_custom_call" | custom-call | tf_op jit(solution)/shard_map/interior/pallas_call | solution.py:350
  15.2 9.9 %gather.1.xyz = f32[4,3,64,128]{3,2,1,0:T(8,128)} custom-call(f32[3,64,128]{2,1,0:T(8,128)} %get-tuple-element.7.mine), custom_call_target="tpu_custom_call" | custom-call | tf_op jit(solution)/shard_map/gather/pallas_call | solution.py:366
  25.1 19.5 %reduced.1.post = f32[2,256,256]{2,1,0:T(8,128)} custom-call(f32[4,3,64,128]{3,2,1,0:T(8,128)} %gather.1.xyz, f32[2,256,128]{2,1,0:T(8,128)} %get-tuple-element.6.hh), custom_call_target="tpu_custom_call" | custom-call | tf_op jit(solution)/shard_map/reduced/pallas_call | solution.py:379
  44.6 57.0 %solve.1 = (f32[2,256]{1,0:T(2,128)}, f32[2,256]{1,0:T(2,128)}) custom-call(f32[2,256,256]{2,1,0:T(8,128)} %get-tuple-element.5.gz, f32[2,256,128]{2,1,0:T(8,128)} %get-tuple-element.6.hh, f32[2,256,256]{2,1,0:T(8,128)} %reduced.1.post, f32[2,256]{1,0:T(2,128)} %weight.1, f32[2,256]{1,0:T(2,128)} %right.1), custom_call_target="tpu_custom_call" | custom-call | tf_op jit(solution)/shard_map/solve/pallas_call | solution.py:390
  101.6 0.0 copy-start.1
  101.6 0.7 copy-done.1
  102.3 0.0 copy-start
  102.3 0.6 copy.8
  102.9 0.1 copy-done
  103.0 0.6 copy.9
Async XLA Ops:
  101.6 0.7 copy-start.1
  102.3 0.7 copy-start

commit v2 on v0

v2 whole, which is shorter than its diff:
```python
import functools

import jax
import jax.numpy as jnp
from jax import lax
from jax.experimental import pallas as pl
from jax.experimental.pallas import tpu as pltpu
from jax.sharding import PartitionSpec as P

B = 64
F32 = jnp.float32
BF16 = jnp.bfloat16
MESH = pl.DeviceIdType.MESH
EXACT = lax.Precision.HIGHEST


def mm(a, b):
    return jnp.dot(a, b, precision=EXACT, preferred_element_type=F32)


def mm_nt(a, b):
    return lax.dot_general(a, b, (((1,), (1,)), ((), ())), precision=EXACT, preferred_element_type=F32)


def iota(shape, dim):
    return lax.broadcasted_iota(jnp.int32, shape, dim)


def low_lanes(rows):
    return iota((rows, 2 * B), 1) < B


def swap(x):
    return jnp.concatenate([x[:, B:], x[:, :B]], axis=1)


def block_diag(pack):
    low = low_lanes(B)
    return jnp.concatenate([jnp.where(low, pack, 0.0), jnp.where(low, 0.0, pack)], axis=0)


def twice(x):
    return jnp.concatenate([x, x], axis=0)


def permuted(x):
    return jnp.concatenate([x[:, B : 2 * B], x[:, 3 * B :], x[:, 2 * B : 3 * B], x[:, :B]], axis=1)


def restored(x):
    return jnp.concatenate([x[:, 3 * B :], x[:, :B], x[:, 2 * B : 3 * B], x[:, B : 2 * B]], axis=1)


def row_of(x, j):
    return jnp.broadcast_to(x[j : j + 1], x.shape)


def invert(work, packs):
    shape = (8, 2 * B)
    sub, lane = iota(shape, 0), iota(shape, 1)
    half = jnp.where(lane < B, 0, B)

    def gather(x, at):
        return jnp.take_along_axis(x, at, axis=1, mode="promise_in_bounds")

    def panel(q, carry):
        base = 8 * q
        within = lane - half - base
        inside = jnp.logical_and(within >= 0, within < 8)
        unit = jnp.where(within == sub, 1.0, 0.0)
        at = [half + base + j for j in range(8)]
        rows = pl.ds(pl.multiple_of(base, 8), 8)
        for p in range(packs):
            r = work[p, rows, :]
            g = [gather(r, at[j]) for j in range(8)]
            r = jnp.where(inside, unit, r)
            for j in range(8):
                mine = sub == j
                inverse = 1.0 / row_of(g[j], j)
                scaled = row_of(r, j) * inverse
                r = jnp.where(mine, scaled, r - g[j] * scaled)
                for c in range(j + 1, 8):
                    scaled = row_of(g[c], j) * inverse
                    g[c] = jnp.where(mine, scaled, g[c] - g[j] * scaled)
            new = [row_of(r, j) for j in range(8)]
            for t in range(B // 8):
                tile = work[p, pl.ds(8 * t, 8), :]
                c = [gather(tile, at[j]) * new[j] for j in range(8)]
                total = ((c[0] + c[1]) + (c[2] + c[3])) + ((c[4] + c[5]) + (c[6] + c[7]))
                work[p, pl.ds(8 * t, 8), :] = jnp.where(inside, 0.0, tile) - total
            work[p, rows, :] = r
        return carry

    lax.fori_loop(0, B // 8, panel, 0)


def store_split(high, low, at, value):
    h = value.astype(BF16)
    high[at] = h
    low[at] = (value - h.astype(F32)).astype(BF16)


def apply(row, weights):
    wide = jnp.broadcast_to(row, (16, row.shape[1]))
    high = wide.astype(BF16).astype(F32)
    both = jnp.where(iota(wide.shape, 0) == 0, high, wide - high).astype(BF16)
    out = sum(jnp.dot(both, w, preferred_element_type=F32) for w in weights)
    return out[:1] + out[1:2]


def kernel(
    dims, diag, coup, weight, right, out_x, out_r,
    dch, pch, vec, in_d13, in_p10, in_d20, in_p23, in_vec, work, uq_s, et_s, xy_s,
    w1h, w1l, w2h, w2l, w3h, w3l, basis, edge_in, wbuf, mine, theirs, sums, sums_in,
    gat_send, gat_recv, edge_send, edge_recv, part_sem, sum_send, sum_recv,
):
    nl, ns, ny = dims
    m, s = lax.axis_index("lines"), lax.axis_index("seg")
    core, y_at, z_at = lax.rem(m, 2), lax.rem(m // 2, ny), m // (2 * ny)
    nz = nl // (2 * ny)

    def line_of(seg):
        return lax.rem(lax.rem((seg + 1) // 2, 2) + m, 2)

    b = line_of(s)
    mate = s + 1 - 2 * lax.rem(s, 2)
    partner = (m, mate)
    other = (lax.rem(m - 1 + 2 * b + nl, nl), s)
    others = [lax.rem(s + d, ns) for d in range(1, ns)]

    def near(index):
        return ((z_at * ny + index // 2) * 2 + core, (s // 2) * 2 + lax.rem(index, 2))

    def far(index):
        return (((index // 2) * ny + y_at) * 2 + lax.rem(index, 2), s)

    groups = ((near, 2 * ny, y_at * 2 + lax.rem(s, 2)), (far, 2 * nz, z_at * 2 + core))
    peers = [(m, x) for x in others] + [other]
    for place, size, own in groups:
        peers += [place(lax.rem(own + d, size)) for d in range(1, size)]
    barrier = pltpu.get_barrier_semaphore()
    for peer in peers:
        pl.semaphore_signal(barrier, inc=1, device_id=peer, device_id_type=MESH)

    not_first = iota((4, 2 * B), 0) > 0
    low4 = low_lanes(4)
    for l in range(2):
        for k in range(B // 2):
            cols = pl.ds(2 * B * k, 2 * B)
            edge = coup[l, :, cols]
            before = jnp.concatenate([edge[3:], edge[:3]], axis=0)
            full = diag[l, :, cols] + edge + jnp.where(not_first, before, 0.0)
            full_t, edge_t = swap(full), swap(edge)
            for dst, x, xt, order in ((dch, full, full_t, (2, 3, 0, 1)), (pch, edge, edge_t, (1, 0, 3, 2))):
                mate_x = jnp.concatenate([x[i : i + 1] for i in order], axis=0)
                mate_t = jnp.concatenate([xt[i : i + 1] for i in order], axis=0)
                dst[pl.ds(4 * B * l + 2 * k, 4, stride=B), :] = jnp.where(low4, x, mate_t)
                dst[pl.ds(4 * B * l + 2 * k + 1, 4, stride=B), :] = jnp.where(low4, xt, mate_x)
    vec[...] = jnp.concatenate([permuted(right[...]), permuted(weight[...])], axis=0)
    pl.semaphore_wait(barrier, len(peers))

    sends = []
    chunks = ((dch, 1, in_d13), (pch, 1, in_p10), (dch, 2, in_d20), (pch, 2, in_p23))

    def chunk_copy(i, to, slot, d):
        if i == len(chunks):
            src, dst = vec, in_vec
        else:
            array, e, dst = chunks[i]
            src = array.at[pl.ds(pl.multiple_of(4 * B * line_of(to) + B * e, B), B), :]
        return pltpu.make_async_remote_copy(
            src_ref=src,
            dst_ref=dst.at[slot],
            send_sem=gat_send.at[i, d],
            recv_sem=gat_recv.at[i, slot],
            device_id=(m, to),
            device_id_type=MESH,
        )

    for i in range(len(chunks) + 1):
        for d, to in enumerate(others):
            copy = chunk_copy(i, to, s, d)
            copy.start()
            sends.append(copy)

    def arrived(i):
        if i == len(chunks):
            in_vec[s] = vec[...]
        else:
            array, e, dst = chunks[i]
            dst[s] = array[pl.ds(pl.multiple_of(4 * B * b + B * e, B), B), :]
        for d, origin in enumerate(others):
            chunk_copy(i, origin, origin, d).wait_recv()

    low = low_lanes(B)
    runs = range(ns)
    arrived(0)
    invert(in_d13, ns)
    arrived(1)
    arrived(3)
    for r in runs:
        p10, p23 = in_p10[r], in_p23[r]
        if r == ns - 1:
            p23 = jnp.where(low, p23, 0.0)
        uq = mm(block_diag(in_d13[r]), jnp.concatenate([p10, p23], axis=0))
        uq_s[r] = uq
        a1 = mm(block_diag(p10), twice(uq[:B]))
        a3 = mm(block_diag(p23), twice(uq[B:]))
        if r == 0:
            arrived(2)
        d20 = in_d20[r]
        s2 = d20 - a1[:B] - a3[:B]
        if r % 2 == 0:
            work[r // 2] = s2
        else:
            work[r // 2] = jnp.where(low, work[r // 2], swap(s2))
        et_s[r] = jnp.where(low, swap(a3[:B]), a1[:B])
        xy_s[r] = jnp.where(low, swap(p23 - a3[B:]), d20 - a1[B:])
    arrived(4)
    invert(work, ns // 2)
    zs, zts, ss = [], [], []
    eye = jnp.where(iota((B, 2 * B), 0) + B == iota((B, 2 * B), 1), 1.0, 0.0)
    for r in runs:
        pack = work[r // 2]
        i2 = pack if r % 2 == 0 else swap(pack)
        et = et_s[r]
        ft = mm(i2[:, :B], et)
        cross = mm(et.T, ft)
        xy = xy_s[r] - jnp.where(low, cross[:B], cross[B:])
        zs.append(cross[B:, :B])
        zts.append(cross[:B, B:])
        ss.append(xy)
        uq = uq_s[r]
        ui = jnp.concatenate([uq[:, :B], eye[:, B:]], axis=0)
        t1 = mm(ui, jnp.concatenate([ft, i2[:, :B]], axis=1))
        t2 = mm_nt(t1[:, 2 * B :], ui)
        q0 = jnp.where(low, 0.0, uq[:B])
        q3 = jnp.where(low, swap(uq[B:]), 0.0)
        h = t1[:, : 2 * B] + jnp.concatenate([q0, q3, jnp.zeros((B, 2 * B), F32)], axis=0)
        h = jnp.concatenate([h, eye], axis=0)
        g = t2[: 2 * B, : 2 * B] + block_diag(in_d13[r])
        g = jnp.concatenate([g, t2[2 * B :, : 2 * B], jnp.zeros((B, 2 * B), F32)], axis=0)
        g2 = jnp.concatenate([t2[:, 2 * B :], jnp.zeros((B, B), F32)], axis=0)
        g2 = jnp.concatenate([g2, jnp.zeros((4 * B, B), F32)], axis=1)
        store_split(w1h, w1l, (r, slice(None), slice(0, 2 * B)), g)
        store_split(w1h, w1l, (r, slice(None), slice(2 * B, 4 * B)), g2)
        store_split(w1h, w1l, (r, slice(None), slice(4 * B, 6 * B)), h)
        ht = h.T
        w3h[r] = jnp.zeros((4 * B, 4 * B), BF16)
        w3l[r] = jnp.zeros((4 * B, 4 * B), BF16)
        store_split(w3h, w3l, (r, slice(B * r, B * r + B)), ht[B:])
        if r < ns - 1:
            store_split(w3h, w3l, (r, slice(B * r + B, B * r + 2 * B)), ht[:B])

    def separator(r):
        own = ss[r][:, B:]
        return own if r == 0 else own + ss[r - 1][:, :B]

    s0, s1, s2, s3 = (separator(r) for r in runs)
    work[0] = jnp.concatenate([s0, s3], axis=1)
    invert(work, 1)
    j0, j3 = work[0, :, :B], work[0, :, B:]
    v0, v3 = mm(j0, zs[0]), mm(j3, zts[2])
    s1 = s1 - mm(zts[0], v0)
    s2 = s2 - mm(zs[2], v3)
    work[0] = jnp.concatenate([s1, s2], axis=1)
    invert(work, 1)
    v12, v21 = mm(work[0, :, :B], zs[1]), mm(work[0, :, B:], zts[1])
    work[0] = jnp.concatenate([s1 - mm(zs[1], v21), s2 - mm(zts[1], v12)], axis=1)
    invert(work, 1)
    e11, e22 = work[0, :, :B], work[0, :, B:]
    e12, e21 = mm(v12, e22), mm(v21, e11)
    inner = jnp.concatenate(
        [jnp.concatenate([e11, e12], axis=1), jnp.concatenate([e21, e22], axis=1)], axis=0
    )
    zero = jnp.zeros((B, B), F32)
    v = jnp.concatenate([jnp.concatenate([v0, zero], axis=1), jnp.concatenate([zero, v3], axis=1)], axis=0)
    side = mm(v, inner)
    corner = mm_nt(side, v)
    back = mm_nt(inner, v)
    rows = (
        jnp.concatenate([j0 + corner[:B, :B], side[:B], corner[:B, B:]], axis=1),
        jnp.concatenate([back[:B, :B], inner[:B], back[:B, B:]], axis=1),
        jnp.concatenate([back[B:, :B], inner[B:], back[B:, B:]], axis=1),
        jnp.concatenate([corner[B:, :B], side[B:], j3 + corner[B:, B:]], axis=1),
    )
    for r in runs:
        after = rows[r + 1] if r + 1 < ns else jnp.zeros((B, 4 * B), F32)
        store_split(w2h, w2l, (slice(2 * B * r, 2 * B * r + B),), after)
        store_split(w2h, w2l, (slice(2 * B * r + B, 2 * B * r + 2 * B),), rows[r])

    def solve(t):
        first = [apply(t[r : r + 1], (w1h[r], w1l[r])) for r in runs]
        f = jnp.concatenate([x[:, 4 * B :] for x in first], axis=1)
        u = apply(f, (w2h[...], w2l[...]))
        out = [first[r][:, : 4 * B] + apply(u, (w3h[r], w3l[r])) for r in runs]
        return jnp.concatenate(out, axis=0)

    def exchange(turn, source, targets):
        copies = []
        for side, to in targets:
            copy = pltpu.make_async_remote_copy(
                src_ref=source,
                dst_ref=edge_in.at[turn, side],
                send_sem=edge_send.at[turn, side],
                recv_sem=edge_recv.at[turn, side],
                device_id=to,
                device_id_type=MESH,
            )
            copy.start()
            copies.append(copy)
            sends.append(copy)
        for copy in copies:
            copy.wait_recv()

    w_mate = jnp.concatenate([in_vec[r, pl.ds(2, 1), :] for r in runs], axis=0)
    w_own = jnp.concatenate([in_vec[r, pl.ds(3, 1), :] for r in runs], axis=0)
    wbuf[...] = w_own
    exchange(4, wbuf, ((1, other),))
    w_other = jnp.where(b == 0, edge_in[4, 1], w_own)
    t = jnp.concatenate([in_vec[r, pl.ds(b, 1), :] for r in runs], axis=0)
    ts, ys = [t], []
    basis[4] = t
    for turn in range(4):
        ys.append(solve(ts[turn]))
        basis[turn] = ys[turn]
        exchange(turn, basis.at[turn], ((0, partner), (1, other)))
        ts.append(w_mate * edge_in[turn, 0] + w_other * edge_in[turn, 1])
        basis[5 + turn] = ts[turn + 1]
    for j in range(9):
        mine[pl.ds(j, 1), :] = basis[j, pl.ds(mate, 1), :]
    swap_copy = pltpu.make_async_remote_copy(
        src_ref=mine,
        dst_ref=theirs,
        send_sem=part_sem.at[0],
        recv_sem=part_sem.at[1],
        device_id=partner,
        device_id_type=MESH,
    )
    for i in range(8):
        both = jnp.sum(ys[i // 2] * ts[(i + 1) // 2], axis=0, keepdims=True)
        sums[0, pl.ds(i, 1), :] = both[:, : 2 * B] + both[:, 2 * B :]
    for stage, (place, size, own) in enumerate(groups):
        for d in range(1, size):
            copy = pltpu.make_async_remote_copy(
                src_ref=sums.at[stage],
                dst_ref=sums_in.at[stage, own],
                send_sem=sum_send.at[stage, d],
                recv_sem=sum_recv.at[stage, own],
                device_id=place(lax.rem(own + d, size)),
                device_id_type=MESH,
            )
            copy.start()
            sends.append(copy)
        if stage == 0:
            swap_copy.start()
        sums_in[stage, own] = sums[stage]
        for d in range(1, size):
            origin = lax.rem(own + d, size)
            pltpu.make_async_remote_copy(
                src_ref=sums.at[stage],
                dst_ref=sums_in.at[stage, origin],
                send_sem=sum_send.at[stage, d],
                recv_sem=sum_recv.at[stage, origin],
                device_id=place(origin),
                device_id_type=MESH,
            ).wait_recv()
        total = sums_in[stage, 0]
        for i in range(1, size):
            total = total + sums_in[stage, i]
        sums[stage + 1] = total
    total = jnp.sum(total, axis=1, keepdims=True)
    moments = [total[i : i + 1] for i in range(8)]
    a = [[moments[i + j] for j in range(4)] + [-moments[i + 4]] for i in range(4)]
    for k in range(3):
        inverse = 1.0 / a[k][k]
        for i in range(k + 1, 4):
            ratio = a[i][k] * inverse
            for j in range(k + 1, 5):
                a[i][j] = a[i][j] - ratio * a[k][j]
    d = [None] * 4 + [jnp.ones((1, 1), F32)]
    for k in (3, 2, 1, 0):
        value = a[k][4]
        for j in range(k + 1, 4):
            value = value - a[k][j] * d[j]
        d[k] = value / a[k][k]
    scale = 1.0 / (d[0] + d[1] + d[2] + d[3] + d[4])
    d = [value * scale for value in d]
    c = [None, None, None, d[4]]
    for k in (2, 1, 0):
        c[k] = c[k + 1] + d[k + 1]

    def combine(part):
        x, r = c[0] * part(0), d[0] * part(4)
        for k in range(1, 4):
            x = x + c[k] * part(k)
        for k in range(1, 5):
            r = r + d[k] * part(4 + k)
        return restored(x), restored(r)

    x_mine, r_mine = combine(lambda j: basis[j, pl.ds(s, 1), :])
    swap_copy.wait()
    x_theirs, r_theirs = combine(lambda j: theirs[pl.ds(j, 1), :])
    first = b == 0
    out_x[pl.ds(0, 1), :] = jnp.where(first, x_mine, x_theirs)
    out_x[pl.ds(1, 1), :] = jnp.where(first, x_theirs, x_mine)
    out_r[pl.ds(0, 1), :] = jnp.where(first, r_mine, r_theirs)
    out_r[pl.ds(1, 1), :] = jnp.where(first, r_theirs, r_mine)
    for copy in sends:
        copy.wait_send()


def local(diag_blocks, couplings, cross_weight, right_side):
    nl, ns = lax.axis_size("lines"), lax.axis_size("seg")
    ny = min(4, nl // 2)
    size = max(2 * ny, nl // ny)
    shape = jax.ShapeDtypeStruct
    block = pl.BlockSpec(memory_space=pltpu.VMEM)
    vmem, dma = pltpu.VMEM, pltpu.SemaphoreType.DMA
    return pl.pallas_call(
        functools.partial(kernel, (nl, ns, ny)),
        out_shape=(shape(right_side.shape, F32), shape(right_side.shape, F32)),
        in_specs=[block] * 4,
        out_specs=[block] * 2,
        scratch_shapes=[
            vmem((8 * B, 2 * B), F32),
            vmem((8 * B, 2 * B), F32),
            vmem((4, 4 * B), F32),
            vmem((ns, B, 2 * B), F32),
            vmem((ns, B, 2 * B), F32),
            vmem((ns, B, 2 * B), F32),
            vmem((ns, B, 2 * B), F32),
            vmem((ns, 4, 4 * B), F32),
            vmem((ns // 2, B, 2 * B), F32),
            vmem((ns, 2 * B, 2 * B), F32),
            vmem((ns, B, 2 * B), F32),
            vmem((ns, B, 2 * B), F32),
            vmem((ns, 4 * B, 6 * B), BF16),
            vmem((ns, 4 * B, 6 * B), BF16),
            vmem((8 * B, 4 * B), BF16),
            vmem((8 * B, 4 * B), BF16),
            vmem((ns, 4 * B, 4 * B), BF16),
            vmem((ns, 4 * B, 4 * B), BF16),
            vmem((9, 4, 4 * B), F32),
            vmem((5, 2, 4, 4 * B), F32),
            vmem((4, 4 * B), F32),
            vmem((16, 4 * B), F32),
            vmem((16, 4 * B), F32),
            vmem((3, 8, 2 * B), F32),
            vmem((2, size, 8, 2 * B), F32),
            dma((5, ns)),
            dma((5, ns)),
            dma((5, 2)),
            dma((5, 2)),
            dma((2,)),
            dma((2, size)),
            dma((2, size)),
        ],
        compiler_params=pltpu.CompilerParams(
            collective_id=0, has_side_effects=True, vmem_limit_bytes=40 * 2**20
        ),
        name="line_cg",
    )(diag_blocks, couplings, cross_weight, right_side)


def solution(mesh):
    return jax.shard_map(
        local,
        mesh=mesh,
        in_specs=(
            P("lines", "seg", None),
            P("lines", "seg", None),
            P("lines", "seg"),
            P("lines", "seg"),
        ),
        out_specs=(P("lines", "seg"), P("lines", "seg")),
        check_vma=False,
    )
```

time: 986 us -> 77.1 us (0.08)
  blocking collectives: 558 us -> 0 us
  other arithmetic: 160 us -> 0 us
  starting transfers between devices: 134 us -> 0 us
  Pallas kernels: 0 us -> 72 us
  waiting for transfers between devices: 65.7 us -> 0 us
  matrix products: 44.5 us -> 0 us
  between operations: 11 us -> 0.65 us
    psum x7 -> x0, blocking collectives: 558 us -> none  [the longest x4 329 us: energy_total(): return lax.psum(jnp.sum(residual * search), ('lines', 'seg'))]
    another operation x50 -> x0, other arithmetic: 153 us -> none  [the longest x28 83.2 us: spd_inverse(): lower_factor = jnp.linalg.cholesky(matrix)]
    ppermute x55 -> x0, starting transfers between devices: 134 us -> none  [the longest x38 91.8 us: passed_along(): return lax.ppermute(array, axis, pairs)]
    pallas_call x0 -> x1, Pallas kernels: none -> 72 us  [local(): pl.pallas_call(functools.partial(kernel, (nl, ns, ny)), out_shape=(shape(...]
    ppermute x55 -> x0, waiting for transfers between devices: 65.7 us -> none  [the longest x38 64.5 us: passed_along(): return lax.ppermute(array, axis, pairs)]
    dot_general x190 -> x0, matrix products: 42.4 us -> none  [the longest x52 10.3 us: matvec_plain(): return jnp.einsum('lij,lj->li', left, right, precision=precise)]
  transfers between devices with their start and end apart: 55 -> 0, of which waited for: 39 -> 0; matrix products, arithmetic and copies ran while one was open for 18% -> 0% of each run, Pallas kernels for 0% -> 0%
where the time goes in v2:
time: 77.1 us; the launch traced here: 76.9 us
  Pallas kernels  72 us (93%)
  local copies, waits for them, and re-layouts  4.32 us (6%)
    pallas_call x1, Pallas kernels, local(): pl.pallas_call(functools.partial(kernel, (nl, ns, ny)), out_shape=(shape(...  72 us
    unnamed x10, local copies, waits for them, and re-layouts  4.32 us

profile of v2, /device:TPU:1, one launch (start us, length us, event | category | flops | bytes accessed | tf_op | source)
XLA Modules:
  0.0 76.9 jit_solution(8333102895705623570)
XLA Ops:
  0.6 0.0 copy-start
  0.6 0.9 %copy-done = f32[2,4,4096]{2,1,0:T(4,128)S(1)} copy-done((f32[2,4,4096]{2,1,0:T(4,128)S(1)}, f32[2,4,4096]{2,1,0:T(4,128)}, u32[]{:S(2)}) %copy-start) | copy-done | bytes 131096
  1.5 0.0 copy-start.1
  1.5 0.9 %copy-done.1 = f32[2,4,4096]{2,1,0:T(4,128)S(1)} copy-done((f32[2,4,4096]{2,1,0:T(4,128)S(1)}, f32[2,4,4096]{2,1,0:T(4,128)}, u32[]{:S(2)}) %copy-start.1) | copy-done | bytes 131096
  2.4 0.0 copy-start.2
  2.4 0.7 copy-done.2
  3.1 0.0 copy-start.3
  3.1 0.7 copy-done.3
  3.8 72.0 %line_cg.1 = (f32[2,256]{1,0:T(2,128)S(1)}, f32[2,256]{1,0:T(2,128)S(1)}) custom-call(f32[2,4,4096]{2,1,0:T(4,128)S(1)} %copy-done, f32[2,4,4096]{2,1,0:T(4,128)S(1)} %copy-done.1, f32[2,256]{1,0:T(2,128)S(1)} %copy-done.2, f32[2,256]{1,0:T(2,128)S(1)} %copy-done.3), custom_call_target="tpu_custom_call" | custom-call | tf_op jit(solution)/shard_map/line_cg/pallas_call | solution.py:420
  75.8 0.6 copy.8
  76.4 0.6 copy.9
Async XLA Ops:
  0.6 0.9 %copy-start = (f32[2,4,4096]{2,1,0:T(4,128)S(1)}, f32[2,4,4096]{2,1,0:T(4,128)}, u32[]{:S(2)}) copy-start(f32[2,4,4096]{2,1,0:T(4,128)} %diag.1) | copy-start | bytes 393220
  1.5 0.9 %copy-start.1 = (f32[2,4,4096]{2,1,0:T(4,128)S(1)}, f32[2,4,4096]{2,1,0:T(4,128)}, u32[]{:S(2)}) copy-start(f32[2,4,4096]{2,1,0:T(4,128)} %coup.1) | copy-start | bytes 393220
  2.4 0.7 copy-start.2
  3.1 0.7 copy-start.3

commit v3 on v2

--- a/solution.py
+++ b/solution.py
@@ -58,40 +58,55 @@
 def invert(work, packs):
     shape = (8, 2 * B)
     sub, lane = iota(shape, 0), iota(shape, 1)
-    half = jnp.where(lane < B, 0, B)
+    low = lane < B
+    half = jnp.where(low, 0, B)
+    lane_all = iota((B, 2 * B), 1)
+    half_all = jnp.where(lane_all < B, 0, B)
+    none = jnp.zeros(shape, F32)
+    every = range(packs)
 
     def gather(x, at):
-        return jnp.take_along_axis(x, at, axis=1, mode="promise_in_bounds")
-
-    def panel(q, carry):
+        return [jnp.take_along_axis(x, i, axis=1, mode="promise_in_bounds") for i in at]
+
+    whole = [work[p] for p in every]
+    rows = [x[:8] for x in whole]
+    for q in range(B // 8):
         base = 8 * q
         within = lane - half - base
         inside = jnp.logical_and(within >= 0, within < 8)
-        unit = jnp.where(within == sub, 1.0, 0.0)
+        within_all = lane_all - half_all - base
+        inside_all = jnp.logical_and(within_all >= 0, within_all < 8)
         at = [half + base + j for j in range(8)]
-        rows = pl.ds(pl.multiple_of(base, 8), 8)
-        for p in range(packs):
-            r = work[p, rows, :]
-            g = [gather(r, at[j]) for j in range(8)]
-            r = jnp.where(inside, unit, r)
-            for j in range(8):
-                mine = sub == j
+        cols = [gather(r, at) for r in rows]
+        more = q + 1 < B // 8
+        if more:
+            after = [x[base + 8 : base + 16] for x in whole]
+            after_cols = [gather(x, at) for x in after]
+        rows = [jnp.where(inside, jnp.where(within == sub, 1.0, 0.0), r) for r in rows]
+        scale = [none for _ in every]
+        for j in range(8):
+            mine = sub == j
+            for p in every:
+                g = cols[p]
                 inverse = 1.0 / row_of(g[j], j)
-                scaled = row_of(r, j) * inverse
-                r = jnp.where(mine, scaled, r - g[j] * scaled)
+                ratio = jnp.where(mine, 0.0, g[j]) * inverse
+                scale[p] = jnp.where(mine, inverse, scale[p])
                 for c in range(j + 1, 8):
-                    scaled = row_of(g[c], j) * inverse
-                    g[c] = jnp.where(mine, scaled, g[c] - g[j] * scaled)
-            new = [row_of(r, j) for j in range(8)]
-            for t in range(B // 8):
-                tile = work[p, pl.ds(8 * t, 8), :]
-                c = [gather(tile, at[j]) * new[j] for j in range(8)]
+                    g[c] = g[c] - ratio * row_of(g[c], j)
+                rows[p] = rows[p] - ratio * row_of(rows[p], j)
+        for p in every:
+            new = rows[p] * scale[p]
+            left, right = jnp.where(low, new, 0.0), jnp.where(low, 0.0, new)
+            weights = jnp.concatenate([none] * q + [left] + [none] * 7 + [right] + [none] * (7 - q), axis=0)
+            rest = jnp.where(inside_all, 0.0, whole[p]) - mm(jnp.where(inside_all, whole[p], 0.0), weights)
+            parts = ([rest[:base]] if q else []) + [new] + ([rest[base + 8 :]] if more else [])
+            whole[p] = jnp.concatenate(parts, axis=0)
+            if more:
+                c = [after_cols[p][j] * row_of(new, j) for j in range(8)]
                 total = ((c[0] + c[1]) + (c[2] + c[3])) + ((c[4] + c[5]) + (c[6] + c[7]))
-                work[p, pl.ds(8 * t, 8), :] = jnp.where(inside, 0.0, tile) - total
-            work[p, rows, :] = r
-        return carry
-
-    lax.fori_loop(0, B // 8, panel, 0)
+                rows[p] = jnp.where(inside, 0.0, after[p]) - total
+    for p in every:
+        work[p] = whole[p]
 
 
 def store_split(high, low, at, value):
@@ -109,7 +124,7 @@
 
 
 def kernel(
-    dims, diag, coup, weight, right, out_x, out_r,
+    dims, diag_in, coup_in, weight_in, right_in, out_x, out_r, diag, coup, weight, right, in_sem,
     dch, pch, vec, in_d13, in_p10, in_d20, in_p23, in_vec, work, uq_s, et_s, xy_s,
     w1h, w1l, w2h, w2l, w3h, w3l, basis, edge_in, wbuf, mine, theirs, sums, sums_in,
     gat_send, gat_recv, edge_send, edge_recv, part_sem, sum_send, sum_recv,
@@ -129,34 +144,44 @@
     others = [lax.rem(s + d, ns) for d in range(1, ns)]
 
     def near(index):
-        return ((z_at * ny + index // 2) * 2 + core, (s // 2) * 2 + lax.rem(index, 2))
+        return (z_at * ny * 2 + index // 2, (s // 2) * 2 + lax.rem(index, 2))
 
     def far(index):
-        return (((index // 2) * ny + y_at) * 2 + lax.rem(index, 2), s)
-
-    groups = ((near, 2 * ny, y_at * 2 + lax.rem(s, 2)), (far, 2 * nz, z_at * 2 + core))
+        return ((index * ny + y_at) * 2 + core, s)
+
+    groups = ((near, 4 * ny, (y_at * 2 + core) * 2 + lax.rem(s, 2)), (far, nz, z_at))
     peers = [(m, x) for x in others] + [other]
     for place, size, own in groups:
         peers += [place(lax.rem(own + d, size)) for d in range(1, size)]
+    pairs = ((diag_in, diag), (coup_in, coup), (weight_in, weight), (right_in, right))
+    loads = [pltpu.make_async_copy(src, dst, in_sem.at[i]) for i, (src, dst) in enumerate(pairs)]
+    for load in loads:
+        load.start()
     barrier = pltpu.get_barrier_semaphore()
     for peer in peers:
         pl.semaphore_signal(barrier, inc=1, device_id=peer, device_id_type=MESH)
 
     not_first = iota((4, 2 * B), 0) > 0
     low4 = low_lanes(4)
-    for l in range(2):
-        for k in range(B // 2):
-            cols = pl.ds(2 * B * k, 2 * B)
-            edge = coup[l, :, cols]
-            before = jnp.concatenate([edge[3:], edge[:3]], axis=0)
-            full = diag[l, :, cols] + edge + jnp.where(not_first, before, 0.0)
-            full_t, edge_t = swap(full), swap(edge)
-            for dst, x, xt, order in ((dch, full, full_t, (2, 3, 0, 1)), (pch, edge, edge_t, (1, 0, 3, 2))):
+
+    def lay_out(dst, tile_of, order):
+        for l in range(2):
+            for k in range(B // 2):
+                x = tile_of(l, pl.ds(2 * B * k, 2 * B))
+                xt = swap(x)
                 mate_x = jnp.concatenate([x[i : i + 1] for i in order], axis=0)
                 mate_t = jnp.concatenate([xt[i : i + 1] for i in order], axis=0)
                 dst[pl.ds(4 * B * l + 2 * k, 4, stride=B), :] = jnp.where(low4, x, mate_t)
                 dst[pl.ds(4 * B * l + 2 * k + 1, 4, stride=B), :] = jnp.where(low4, xt, mate_x)
-    vec[...] = jnp.concatenate([permuted(right[...]), permuted(weight[...])], axis=0)
+
+    def diagonal(l, cols):
+        edge = coup[l, :, cols]
+        before = jnp.concatenate([edge[3:], edge[:3]], axis=0)
+        return diag[l, :, cols] + edge + jnp.where(not_first, before, 0.0)
+
+    loads[0].wait()
+    loads[1].wait()
+    lay_out(dch, diagonal, (2, 3, 0, 1))
     pl.semaphore_wait(barrier, len(peers))
 
     sends = []
@@ -177,11 +202,21 @@
             device_id_type=MESH,
         )
 
-    for i in range(len(chunks) + 1):
+    def send_chunk(i):
         for d, to in enumerate(others):
             copy = chunk_copy(i, to, s, d)
             copy.start()
             sends.append(copy)
+
+    send_chunk(0)
+    lay_out(pch, lambda l, cols: coup[l, :, cols], (1, 0, 3, 2))
+    send_chunk(1)
+    send_chunk(3)
+    loads[2].wait()
+    loads[3].wait()
+    vec[...] = jnp.concatenate([permuted(right[...]), permuted(weight[...])], axis=0)
+    send_chunk(4)
+    send_chunk(2)
 
     def arrived(i):
         if i == len(chunks):
@@ -191,6 +226,27 @@
             dst[s] = array[pl.ds(pl.multiple_of(4 * B * b + B * e, B), B), :]
         for d, origin in enumerate(others):
             chunk_copy(i, origin, origin, d).wait_recv()
+
+    def exchange(turn, source, targets):
+        copies = []
+        for side, to in targets:
+            copy = pltpu.make_async_remote_copy(
+                src_ref=source,
+                dst_ref=edge_in.at[turn, side],
+                send_sem=edge_send.at[turn, side],
+                recv_sem=edge_recv.at[turn, side],
+                device_id=to,
+                device_id_type=MESH,
+            )
+            copy.start()
+            copies.append(copy)
+            sends.append(copy)
+
+        def finish():
+            for copy in copies:
+                copy.wait_recv()
+
+        return finish
 
     low = low_lanes(B)
     runs = range(ns)
@@ -217,6 +273,10 @@
         et_s[r] = jnp.where(low, swap(a3[:B]), a1[:B])
         xy_s[r] = jnp.where(low, swap(p23 - a3[B:]), d20 - a1[B:])
     arrived(4)
+    w_mate = jnp.concatenate([in_vec[r, pl.ds(2, 1), :] for r in runs], axis=0)
+    w_own = jnp.concatenate([in_vec[r, pl.ds(3, 1), :] for r in runs], axis=0)
+    wbuf[...] = w_own
+    wait_weights = exchange(4, wbuf, ((1, other),))
     invert(work, ns // 2)
     zs, zts, ss = [], [], []
     eye = jnp.where(iota((B, 2 * B), 0) + B == iota((B, 2 * B), 1), 1.0, 0.0)
@@ -296,35 +356,17 @@
         out = [first[r][:, : 4 * B] + apply(u, (w3h[r], w3l[r])) for r in runs]
         return jnp.concatenate(out, axis=0)
 
-    def exchange(turn, source, targets):
-        copies = []
-        for side, to in targets:
-            copy = pltpu.make_async_remote_copy(
-                src_ref=source,
-                dst_ref=edge_in.at[turn, side],
-                send_sem=edge_send.at[turn, side],
-                recv_sem=edge_recv.at[turn, side],
-                device_id=to,
-                device_id_type=MESH,
-            )
-            copy.start()
-            copies.append(copy)
-            sends.append(copy)
-        for copy in copies:
-            copy.wait_recv()
-
-    w_mate = jnp.concatenate([in_vec[r, pl.ds(2, 1), :] for r in runs], axis=0)
-    w_own = jnp.concatenate([in_vec[r, pl.ds(3, 1), :] for r in runs], axis=0)
-    wbuf[...] = w_own
-    exchange(4, wbuf, ((1, other),))
-    w_other = jnp.where(b == 0, edge_in[4, 1], w_own)
     t = jnp.concatenate([in_vec[r, pl.ds(b, 1), :] for r in runs], axis=0)
     ts, ys = [t], []
     basis[4] = t
     for turn in range(4):
         ys.append(solve(ts[turn]))
         basis[turn] = ys[turn]
-        exchange(turn, basis.at[turn], ((0, partner), (1, other)))
+        arrive = exchange(turn, basis.at[turn], ((0, partner), (1, other)))
+        if turn == 0:
+            wait_weights()
+            w_other = jnp.where(b == 0, edge_in[4, 1], w_own)
+        arrive()
         ts.append(w_mate * edge_in[turn, 0] + w_other * edge_in[turn, 1])
         basis[5 + turn] = ts[turn + 1]
     for j in range(9):
@@ -413,16 +455,21 @@
 def local(diag_blocks, couplings, cross_weight, right_side):
     nl, ns = lax.axis_size("lines"), lax.axis_size("seg")
     ny = min(4, nl // 2)
-    size = max(2 * ny, nl // ny)
+    size = max(4 * ny, nl // (2 * ny))
     shape = jax.ShapeDtypeStruct
     block = pl.BlockSpec(memory_space=pltpu.VMEM)
     vmem, dma = pltpu.VMEM, pltpu.SemaphoreType.DMA
     return pl.pallas_call(
         functools.partial(kernel, (nl, ns, ny)),
         out_shape=(shape(right_side.shape, F32), shape(right_side.shape, F32)),
-        in_specs=[block] * 4,
+        in_specs=[pl.BlockSpec(memory_space=pltpu.HBM)] * 4,
         out_specs=[block] * 2,
         scratch_shapes=[
+            vmem(diag_blocks.shape, F32),
+            vmem(couplings.shape, F32),
+            vmem(cross_weight.shape, F32),
+            vmem(right_side.shape, F32),
+            dma((4,)),
             vmem((8 * B, 2 * B), F32),
             vmem((8 * B, 2 * B), F32),
             vmem((4, 4 * B), F32),
@@ -457,7 +504,7 @@
             dma((2, size)),
         ],
         compiler_params=pltpu.CompilerParams(
-            collective_id=0, has_side_effects=True, vmem_limit_bytes=40 * 2**20
+            collective_id=0, has_side_effects=True
         ),
         name="line_cg",
     )(diag_blocks, couplings, cross_weight, right_side)

time: 77.1 us -> 61.8 us (0.80)
  Pallas kernels: 72 us -> 58.4 us
  local copies, waits for them, and re-layouts: 4.32 us -> 1.89 us
    pallas_call x1, Pallas kernels: 72 us -> 58.4 us  [local(): pl.pallas_call(functools.partial(kernel, (nl, ns, ny)), out_shape=(shape(...]
    unnamed x10 -> x6, local copies, waits for them, and re-layouts: 4.32 us -> 1.89 us
where the time goes in v3:
time: 61.8 us; the launch traced here: 60.9 us
  Pallas kernels  58.4 us (94%)
  local copies, waits for them, and re-layouts  1.89 us (3%)
  between operations  0.65 us (1%)
    pallas_call x1, Pallas kernels, local(): pl.pallas_call(functools.partial(kernel, (nl, ns, ny)), out_shape=(shape(...  58.4 us
    unnamed x6, local copies, waits for them, and re-layouts  1.89 us

profile of v3, /device:TPU:1, one launch (start us, length us, event | category | flops | bytes accessed | tf_op | source)
XLA Modules:
  0.0 60.9 jit_solution(6686836648705998516)
XLA Ops:
  0.6 58.4 %line_cg.1 = (f32[2,256]{1,0:T(2,128)}, f32[2,256]{1,0:T(2,128)}) custom-call(f32[2,4,4096]{2,1,0:T(4,128)} %diag_in.1, f32[2,4,4096]{2,1,0:T(4,128)} %coup_in.1, f32[2,256]{1,0:T(2,128)} %weight_in.1, f32[2,256]{1,0:T(2,128)} %right_in.1), custom_call_target="tpu_custom_call" | custom-call | tf_op jit(solution)/shard_map/line_cg/pallas_call | solution.py:462
  59.0 0.0 copy-start.1
  59.0 0.7 %copy-done.1 = f32[2,256]{1,0:T(2,128)S(1)} copy-done((f32[2,256]{1,0:T(2,128)S(1)}, f32[2,256]{1,0:T(2,128)}, u32[]{:S(2)}) %copy-start.1) | copy-done | bytes 2072
  59.7 0.0 copy-start
  59.7 0.6 copy.8
  60.2 0.1 copy-done
  60.3 0.6 copy.9
Async XLA Ops:
  59.0 0.7 %copy-start.1 = (f32[2,256]{1,0:T(2,128)S(1)}, f32[2,256]{1,0:T(2,128)}, u32[]{:S(2)}) copy-start(f32[2,256]{1,0:T(2,128)} %get-tuple-element.4) | copy-start | bytes 6148
  59.7 0.7 %copy-start = (f32[2,256]{1,0:T(2,128)S(1)}, f32[2,256]{1,0:T(2,128)}, u32[]{:S(2)}) copy-start(f32[2,256]{1,0:T(2,128)} %get-tuple-element.5) | copy-start | bytes 6148

commit v4 on v3

--- a/solution.py
+++ b/solution.py
@@ -67,6 +67,11 @@
 
     def gather(x, at):
         return [jnp.take_along_axis(x, i, axis=1, mode="promise_in_bounds") for i in at]
+
+    def less(x, x_cols, new, inside):
+        c = [x_cols[j] * row_of(new, j) for j in range(8)]
+        total = ((c[0] + c[1]) + (c[2] + c[3])) + ((c[4] + c[5]) + (c[6] + c[7]))
+        return jnp.where(inside, 0.0, x) - total
 
     whole = [work[p] for p in every]
     rows = [x[:8] for x in whole]
@@ -102,9 +107,7 @@
             parts = ([rest[:base]] if q else []) + [new] + ([rest[base + 8 :]] if more else [])
             whole[p] = jnp.concatenate(parts, axis=0)
             if more:
-                c = [after_cols[p][j] * row_of(new, j) for j in range(8)]
-                total = ((c[0] + c[1]) + (c[2] + c[3])) + ((c[4] + c[5]) + (c[6] + c[7]))
-                rows[p] = jnp.where(inside, 0.0, after[p]) - total
+                rows[p] = less(after[p], after_cols[p], new, inside)
     for p in every:
         work[p] = whole[p]
 
@@ -124,10 +127,11 @@
 
 
 def kernel(
-    dims, diag_in, coup_in, weight_in, right_in, out_x, out_r, diag, coup, weight, right, in_sem,
+    dims, diag_in, coup_in, weight_in, right_in, out, diag, coup, weight, right, in_sem,
     dch, pch, vec, in_d13, in_p10, in_d20, in_p23, in_vec, work, uq_s, et_s, xy_s,
-    w1h, w1l, w2h, w2l, w3h, w3l, basis, edge_in, wbuf, mine, theirs, sums, sums_in,
-    gat_send, gat_recv, edge_send, edge_recv, part_sem, sum_send, sum_recv,
+    w1h, w1l, w2h, w2l, w3h, w3l, basis, edge_in, wbuf, wline, plane_w, note, notes, ahead, mine, theirs, sums, sums_in,
+    gat_send, gat_recv, edge_send, edge_recv, pw_send, pw_recv, note_send, note_recv, ahead_send, ahead_recv,
+    part_sem, sum_send, sum_recv,
 ):
     nl, ns, ny = dims
     m, s = lax.axis_index("lines"), lax.axis_index("seg")
@@ -144,15 +148,25 @@
     others = [lax.rem(s + d, ns) for d in range(1, ns)]
 
     def near(index):
-        return (z_at * ny * 2 + index // 2, (s // 2) * 2 + lax.rem(index, 2))
+        at, turned = index // 2, lax.rem(index + index // 2, 2)
+        return (z_at * ny * 2 + at, (s // 2) * (3 - 2 * turned) + turned)
 
     def far(index):
         return ((index * ny + y_at) * 2 + core, s)
 
-    groups = ((near, 4 * ny, (y_at * 2 + core) * 2 + lax.rem(s, 2)), (far, nz, z_at))
-    peers = [(m, x) for x in others] + [other]
-    for place, size, own in groups:
+    groups = ((near, 4 * ny, (y_at * 2 + core) * 2 + b), (far, nz, z_at))
+    many, rank = groups[0][1:]
+    step = 2 * ny
+
+    def shifted(place, by):
+        return (lax.rem(place[0] + by + nl, nl), place[1])
+
+    herald = shifted(near(0), step)
+    sends_across = rank == 0
+    peers = [(m, x) for x in others]
+    for place, size, own in groups[::-1]:
         peers += [place(lax.rem(own + d, size)) for d in range(1, size)]
+    peers += [other, herald]
     pairs = ((diag_in, diag), (coup_in, coup), (weight_in, weight), (right_in, right))
     loads = [pltpu.make_async_copy(src, dst, in_sem.at[i]) for i, (src, dst) in enumerate(pairs)]
     for load in loads:
@@ -160,6 +174,11 @@
     barrier = pltpu.get_barrier_semaphore()
     for peer in peers:
         pl.semaphore_signal(barrier, inc=1, device_id=peer, device_id_type=MESH)
+
+    @pl.when(sends_across)
+    def _():
+        for i in range(many):
+            pl.semaphore_signal(barrier, inc=1, device_id=shifted(near(i), -step), device_id_type=MESH)
 
     not_first = iota((4, 2 * B), 0) > 0
     low4 = low_lanes(4)
@@ -182,7 +201,7 @@
     loads[0].wait()
     loads[1].wait()
     lay_out(dch, diagonal, (2, 3, 0, 1))
-    pl.semaphore_wait(barrier, len(peers))
+    pl.semaphore_wait(barrier, len(peers) + jnp.where(sends_across, many, 0))
 
     sends = []
     chunks = ((dch, 1, in_d13), (pch, 1, in_p10), (dch, 2, in_d20), (pch, 2, in_p23))
@@ -245,6 +264,34 @@
         def finish():
             for copy in copies:
                 copy.wait_recv()
+
+        return finish
+
+    def spread(place, size, own, source, inbox, send_sem, recv_sem):
+        for d in range(1, size):
+            copy = pltpu.make_async_remote_copy(
+                src_ref=source,
+                dst_ref=inbox.at[own],
+                send_sem=send_sem.at[d],
+                recv_sem=recv_sem.at[own],
+                device_id=place(lax.rem(own + d, size)),
+                device_id_type=MESH,
+            )
+            copy.start()
+            sends.append(copy)
+        inbox[own] = source[...]
+
+        def finish():
+            for d in range(1, size):
+                origin = lax.rem(own + d, size)
+                pltpu.make_async_remote_copy(
+                    src_ref=source,
+                    dst_ref=inbox.at[origin],
+                    send_sem=send_sem.at[d],
+                    recv_sem=recv_sem.at[origin],
+                    device_id=place(origin),
+                    device_id_type=MESH,
+                ).wait_recv()
 
         return finish
 
@@ -356,19 +403,81 @@
         out = [first[r][:, : 4 * B] + apply(u, (w3h[r], w3l[r])) for r in runs]
         return jnp.concatenate(out, axis=0)
 
+    def folded(x):
+        x = jnp.sum(x, axis=0, keepdims=True)
+        return x[:, : 2 * B] + x[:, 2 * B :]
+
+    def moment(i):
+        note[4 + i // 2 : 5 + i // 2, 2 * B * (i % 2) : 2 * B * (i % 2) + 2 * B] = folded(
+            ys[i // 2] * ts[(i + 1) // 2]
+        )
+
+    note[7:8, 2 * B :] = jnp.zeros((1, 2 * B), F32)
     t = jnp.concatenate([in_vec[r, pl.ds(b, 1), :] for r in runs], axis=0)
     ts, ys = [t], []
     basis[4] = t
     for turn in range(4):
         ys.append(solve(ts[turn]))
         basis[turn] = ys[turn]
+        if turn == 3:
+            break
         arrive = exchange(turn, basis.at[turn], ((0, partner), (1, other)))
         if turn == 0:
+            wline[...] = jnp.where(b == 0, w_mate, w_own)
+            wait_plane = spread(near, many, rank, wline, plane_w, pw_send, pw_recv)
             wait_weights()
             w_other = jnp.where(b == 0, edge_in[4, 1], w_own)
+        moment(2 * turn)
+        if turn:
+            moment(2 * turn - 1)
         arrive()
         ts.append(w_mate * edge_in[turn, 0] + w_other * edge_in[turn, 1])
         basis[5 + turn] = ts[turn + 1]
+
+    note[0:4, :] = ys[3]
+    moment(5)
+    moment(6)
+    wait_notes = spread(near, many, rank, note, notes, note_send, note_recv)
+
+    def across(to):
+        return pltpu.make_async_remote_copy(
+            src_ref=note.at[...],
+            dst_ref=ahead,
+            send_sem=ahead_send.at[to],
+            recv_sem=ahead_recv.at[0],
+            device_id=shifted(near(to), -step),
+            device_id_type=MESH,
+        )
+
+    @pl.when(sends_across)
+    def _():
+        for i in range(many):
+            across(i).start()
+
+    arrive = exchange(3, basis.at[3], ((0, partner), (1, other)))
+    wait_plane()
+    wait_notes()
+    pltpu.make_async_remote_copy(
+        src_ref=note.at[...],
+        dst_ref=ahead,
+        send_sem=ahead_send.at[0],
+        recv_sem=ahead_recv.at[0],
+        device_id=herald,
+        device_id_type=MESH,
+    ).wait_recv()
+    last = jnp.zeros((ns, 4 * B), F32)
+    total = jnp.zeros((ns, 4 * B), F32)
+    for i in range(many):
+        following = notes[i + 1, 0:4, :] if i + 1 < many else ahead[0:4, :]
+        last = last + plane_w[i] * notes[i, 0:4, :] * following
+        total = total + notes[i, 4:8, :]
+    last = 2.0 * folded(last)
+    for i in range(8):
+        sums[pl.ds(i, 1), :] = last if i == 7 else total[i // 2 : i // 2 + 1, 2 * B * (i % 2) : 2 * B * (i % 2) + 2 * B]
+    wait_sums = spread(far, nz, z_at, sums, sums_in, sum_send, sum_recv)
+    arrive()
+    ts.append(w_mate * edge_in[3, 0] + w_other * edge_in[3, 1])
+    basis[8] = ts[4]
     for j in range(9):
         mine[pl.ds(j, 1), :] = basis[j, pl.ds(mate, 1), :]
     swap_copy = pltpu.make_async_remote_copy(
@@ -379,38 +488,11 @@
         device_id=partner,
         device_id_type=MESH,
     )
-    for i in range(8):
-        both = jnp.sum(ys[i // 2] * ts[(i + 1) // 2], axis=0, keepdims=True)
-        sums[0, pl.ds(i, 1), :] = both[:, : 2 * B] + both[:, 2 * B :]
-    for stage, (place, size, own) in enumerate(groups):
-        for d in range(1, size):
-            copy = pltpu.make_async_remote_copy(
-                src_ref=sums.at[stage],
-                dst_ref=sums_in.at[stage, own],
-                send_sem=sum_send.at[stage, d],
-                recv_sem=sum_recv.at[stage, own],
-                device_id=place(lax.rem(own + d, size)),
-                device_id_type=MESH,
-            )
-            copy.start()
-            sends.append(copy)
-        if stage == 0:
-            swap_copy.start()
-        sums_in[stage, own] = sums[stage]
-        for d in range(1, size):
-            origin = lax.rem(own + d, size)
-            pltpu.make_async_remote_copy(
-                src_ref=sums.at[stage],
-                dst_ref=sums_in.at[stage, origin],
-                send_sem=sum_send.at[stage, d],
-                recv_sem=sum_recv.at[stage, origin],
-                device_id=place(origin),
-                device_id_type=MESH,
-            ).wait_recv()
-        total = sums_in[stage, 0]
-        for i in range(1, size):
-            total = total + sums_in[stage, i]
-        sums[stage + 1] = total
+    swap_copy.start()
+    wait_sums()
+    total = sums_in[0]
+    for i in range(1, nz):
+        total = total + sums_in[i]
     total = jnp.sum(total, axis=1, keepdims=True)
     moments = [total[i : i + 1] for i in range(8)]
     a = [[moments[i + j] for j in range(4)] + [-moments[i + 4]] for i in range(4)]
@@ -444,26 +526,31 @@
     swap_copy.wait()
     x_theirs, r_theirs = combine(lambda j: theirs[pl.ds(j, 1), :])
     first = b == 0
-    out_x[pl.ds(0, 1), :] = jnp.where(first, x_mine, x_theirs)
-    out_x[pl.ds(1, 1), :] = jnp.where(first, x_theirs, x_mine)
-    out_r[pl.ds(0, 1), :] = jnp.where(first, r_mine, r_theirs)
-    out_r[pl.ds(1, 1), :] = jnp.where(first, r_theirs, r_mine)
+    out[pl.ds(0, 1), :] = jnp.where(first, x_mine, x_theirs)
+    out[pl.ds(1, 1), :] = jnp.where(first, x_theirs, x_mine)
+    out[pl.ds(2, 1), :] = jnp.where(first, r_mine, r_theirs)
+    out[pl.ds(3, 1), :] = jnp.where(first, r_theirs, r_mine)
     for copy in sends:
         copy.wait_send()
+
+    @pl.when(sends_across)
+    def _():
+        for i in range(many):
+            across(i).wait_send()
 
 
 def local(diag_blocks, couplings, cross_weight, right_side):
     nl, ns = lax.axis_size("lines"), lax.axis_size("seg")
     ny = min(4, nl // 2)
-    size = max(4 * ny, nl // (2 * ny))
+    nz, many = nl // (2 * ny), 4 * ny
     shape = jax.ShapeDtypeStruct
     block = pl.BlockSpec(memory_space=pltpu.VMEM)
     vmem, dma = pltpu.VMEM, pltpu.SemaphoreType.DMA
-    return pl.pallas_call(
+    out = pl.pallas_call(
         functools.partial(kernel, (nl, ns, ny)),
-        out_shape=(shape(right_side.shape, F32), shape(right_side.shape, F32)),
+        out_shape=shape((4, 4 * B), F32),
         in_specs=[pl.BlockSpec(memory_space=pltpu.HBM)] * 4,
-        out_specs=[block] * 2,
+        out_specs=block,
         scratch_shapes=[
             vmem(diag_blocks.shape, F32),
             vmem(couplings.shape, F32),
@@ -491,23 +578,35 @@
             vmem((9, 4, 4 * B), F32),
             vmem((5, 2, 4, 4 * B), F32),
             vmem((4, 4 * B), F32),
+            vmem((4, 4 * B), F32),
+            vmem((many, 4, 4 * B), F32),
+            vmem((8, 4 * B), F32),
+            vmem((many, 8, 4 * B), F32),
+            vmem((8, 4 * B), F32),
             vmem((16, 4 * B), F32),
             vmem((16, 4 * B), F32),
-            vmem((3, 8, 2 * B), F32),
-            vmem((2, size, 8, 2 * B), F32),
+            vmem((8, 2 * B), F32),
+            vmem((nz, 8, 2 * B), F32),
             dma((5, ns)),
             dma((5, ns)),
             dma((5, 2)),
             dma((5, 2)),
+            dma((many,)),
+            dma((many,)),
+            dma((many,)),
+            dma((many,)),
+            dma((many,)),
+            dma((1,)),
             dma((2,)),
-            dma((2, size)),
-            dma((2, size)),
+            dma((nz,)),
+            dma((nz,)),
         ],
         compiler_params=pltpu.CompilerParams(
             collective_id=0, has_side_effects=True
         ),
         name="line_cg",
     )(diag_blocks, couplings, cross_weight, right_side)
+    return out[:2], out[2:]
 
 
 def solution(mesh):

time: 61.8 us -> 58 us (0.939); the launches traced: 60.9 us -> 57.9 us
  Pallas kernels: 58.4 us -> 55.9 us
    pallas_call x1, Pallas kernels: 58.4 us -> 55.9 us  [local(): pl.pallas_call(functools.partial(kernel, (nl, ns, ny)), out_shape=shape((...]
    unnamed x6 -> x0, local copies, waits for them, and re-layouts: 1.89 us -> none
    slice x0 -> x1, local copies, waits for them, and re-layouts: none -> 1.33 us  [local(): return (out[:2], out[2:])]
where the time goes in v4:
time: 58 us; the launch traced here: 57.9 us
  Pallas kernels  55.9 us (96%)
  local copies, waits for them, and re-layouts  1.33 us (2%)
  between operations  0.64 us (1%)
    pallas_call x1, Pallas kernels, local(): pl.pallas_call(functools.partial(kernel, (nl, ns, ny)), out_shape=shape((...  55.9 us
    slice x1, local copies, waits for them, and re-layouts, local(): return (out[:2], out[2:])  1.33 us

profile of v4, /device:TPU:1, one launch (start us, length us, event | category | flops | bytes accessed | tf_op | source)
XLA Modules:
  0.0 57.9 jit_solution(3848673007256757258)
XLA Ops:
  0.6 55.9 %line_cg.1 = f32[4,256]{1,0:T(4,128)} custom-call(f32[2,4,4096]{2,1,0:T(4,128)} %diag_in.1, f32[2,4,4096]{2,1,0:T(4,128)} %coup_in.1, f32[2,256]{1,0:T(2,128)} %weight_in.1, f32[2,256]{1,0:T(2,128)} %right_in.1), custom_call_target="tpu_custom_call" | custom-call | tf_op jit(solution)/shard_map/line_cg/pallas_call | solution.py:549
  56.5 1.3 %fusion = (f32[2,256]{1,0:T(2,128)}, f32[2,256]{1,0:T(2,128)}) fusion(f32[4,256]{1,0:T(4,128)} %line_cg.1), kind=kLoop, calls=%fused_computation | loop fusion | bytes 8192 | tf_op jit(solution)/shard_map/slice | solution.py:609

commit v5 on v4

--- a/solution.py
+++ b/solution.py
@@ -55,7 +55,7 @@
     return jnp.broadcast_to(x[j : j + 1], x.shape)
 
 
-def invert(work, packs):
+def invert(work, packs, beside=iter(())):
     shape = (8, 2 * B)
     sub, lane = iota(shape, 0), iota(shape, 1)
     low = lane < B
@@ -76,6 +76,7 @@
     whole = [work[p] for p in every]
     rows = [x[:8] for x in whole]
     for q in range(B // 8):
+        next(beside, None)
         base = 8 * q
         within = lane - half - base
         inside = jnp.logical_and(within >= 0, within < 8)
@@ -169,11 +170,12 @@
     peers += [other, herald]
     pairs = ((diag_in, diag), (coup_in, coup), (weight_in, weight), (right_in, right))
     loads = [pltpu.make_async_copy(src, dst, in_sem.at[i]) for i, (src, dst) in enumerate(pairs)]
-    for load in loads:
-        load.start()
     barrier = pltpu.get_barrier_semaphore()
     for peer in peers:
         pl.semaphore_signal(barrier, inc=1, device_id=peer, device_id_type=MESH)
+
+    for load in loads:
+        load.start()
 
     @pl.when(sends_across)
     def _():
@@ -325,39 +327,56 @@
     wbuf[...] = w_own
     wait_weights = exchange(4, wbuf, ((1, other),))
     invert(work, ns // 2)
-    zs, zts, ss = [], [], []
+    zs, zts, ss, fts, i2s = [], [], [], [], []
     eye = jnp.where(iota((B, 2 * B), 0) + B == iota((B, 2 * B), 1), 1.0, 0.0)
     for r in runs:
         pack = work[r // 2]
-        i2 = pack if r % 2 == 0 else swap(pack)
+        i2 = (pack if r % 2 == 0 else swap(pack))[:, :B]
         et = et_s[r]
-        ft = mm(i2[:, :B], et)
+        ft = mm(i2, et)
         cross = mm(et.T, ft)
         xy = xy_s[r] - jnp.where(low, cross[:B], cross[B:])
         zs.append(cross[B:, :B])
         zts.append(cross[:B, B:])
         ss.append(xy)
-        uq = uq_s[r]
-        ui = jnp.concatenate([uq[:, :B], eye[:, B:]], axis=0)
-        t1 = mm(ui, jnp.concatenate([ft, i2[:, :B]], axis=1))
-        t2 = mm_nt(t1[:, 2 * B :], ui)
-        q0 = jnp.where(low, 0.0, uq[:B])
-        q3 = jnp.where(low, swap(uq[B:]), 0.0)
-        h = t1[:, : 2 * B] + jnp.concatenate([q0, q3, jnp.zeros((B, 2 * B), F32)], axis=0)
-        h = jnp.concatenate([h, eye], axis=0)
-        g = t2[: 2 * B, : 2 * B] + block_diag(in_d13[r])
-        g = jnp.concatenate([g, t2[2 * B :, : 2 * B], jnp.zeros((B, 2 * B), F32)], axis=0)
-        g2 = jnp.concatenate([t2[:, 2 * B :], jnp.zeros((B, B), F32)], axis=0)
-        g2 = jnp.concatenate([g2, jnp.zeros((4 * B, B), F32)], axis=1)
-        store_split(w1h, w1l, (r, slice(None), slice(0, 2 * B)), g)
-        store_split(w1h, w1l, (r, slice(None), slice(2 * B, 4 * B)), g2)
-        store_split(w1h, w1l, (r, slice(None), slice(4 * B, 6 * B)), h)
-        ht = h.T
-        w3h[r] = jnp.zeros((4 * B, 4 * B), BF16)
-        w3l[r] = jnp.zeros((4 * B, 4 * B), BF16)
-        store_split(w3h, w3l, (r, slice(B * r, B * r + B)), ht[B:])
-        if r < ns - 1:
-            store_split(w3h, w3l, (r, slice(B * r + B, B * r + 2 * B)), ht[:B])
+        fts.append(ft)
+        i2s.append(i2)
+
+    t = jnp.concatenate([in_vec[r, pl.ds(b, 1), :] for r in runs], axis=0)
+    begun = []
+
+    def operators():
+        for r in runs:
+            uq = uq_s[r]
+            ui = jnp.concatenate([uq[:, :B], eye[:, B:]], axis=0)
+            t1 = mm(ui, jnp.concatenate([fts[r], i2s[r]], axis=1))
+            yield
+            q0 = jnp.where(low, 0.0, uq[:B])
+            q3 = jnp.where(low, swap(uq[B:]), 0.0)
+            h = t1[:, : 2 * B] + jnp.concatenate([q0, q3, jnp.zeros((B, 2 * B), F32)], axis=0)
+            h = jnp.concatenate([h, eye], axis=0)
+            store_split(w1h, w1l, (r, slice(None), slice(4 * B, 6 * B)), h)
+            yield
+            t2 = mm_nt(t1[:, 2 * B :], ui)
+            g = t2[: 2 * B, : 2 * B] + block_diag(in_d13[r])
+            g = jnp.concatenate([g, t2[2 * B :, : 2 * B], jnp.zeros((B, 2 * B), F32)], axis=0)
+            store_split(w1h, w1l, (r, slice(None), slice(0, 2 * B)), g)
+            yield
+            g = jnp.concatenate([t2[:, 2 * B :], jnp.zeros((B, B), F32)], axis=0)
+            g = jnp.concatenate([g, jnp.zeros((4 * B, B), F32)], axis=1)
+            store_split(w1h, w1l, (r, slice(None), slice(2 * B, 4 * B)), g)
+            yield
+            ht = h.T
+            w3h[r] = jnp.zeros((4 * B, 4 * B), BF16)
+            w3l[r] = jnp.zeros((4 * B, 4 * B), BF16)
+            store_split(w3h, w3l, (r, slice(B * r, B * r + B)), ht[B:])
+            if r < ns - 1:
+                store_split(w3h, w3l, (r, slice(B * r + B, B * r + 2 * B)), ht[:B])
+            yield
+            begun.append(apply(t[r : r + 1], (w1h[r], w1l[r])))
+            yield
+
+    beside = operators()
 
     def separator(r):
         own = ss[r][:, B:]
@@ -365,16 +384,18 @@
 
     s0, s1, s2, s3 = (separator(r) for r in runs)
     work[0] = jnp.concatenate([s0, s3], axis=1)
-    invert(work, 1)
+    invert(work, 1, beside)
     j0, j3 = work[0, :, :B], work[0, :, B:]
     v0, v3 = mm(j0, zs[0]), mm(j3, zts[2])
     s1 = s1 - mm(zts[0], v0)
     s2 = s2 - mm(zs[2], v3)
     work[0] = jnp.concatenate([s1, s2], axis=1)
-    invert(work, 1)
+    invert(work, 1, beside)
     v12, v21 = mm(work[0, :, :B], zs[1]), mm(work[0, :, B:], zts[1])
     work[0] = jnp.concatenate([s1 - mm(zs[1], v21), s2 - mm(zts[1], v12)], axis=1)
-    invert(work, 1)
+    invert(work, 1, beside)
+    for _ in beside:
+        pass
     e11, e22 = work[0, :, :B], work[0, :, B:]
     e12, e21 = mm(v12, e22), mm(v21, e11)
     inner = jnp.concatenate(
@@ -396,8 +417,10 @@
         store_split(w2h, w2l, (slice(2 * B * r, 2 * B * r + B),), after)
         store_split(w2h, w2l, (slice(2 * B * r + B, 2 * B * r + 2 * B),), rows[r])
 
-    def solve(t):
-        first = [apply(t[r : r + 1], (w1h[r], w1l[r])) for r in runs]
+    def begin(t):
+        return [apply(t[r : r + 1], (w1h[r], w1l[r])) for r in runs]
+
+    def solve(first):
         f = jnp.concatenate([x[:, 4 * B :] for x in first], axis=1)
         u = apply(f, (w2h[...], w2l[...]))
         out = [first[r][:, : 4 * B] + apply(u, (w3h[r], w3l[r])) for r in runs]
@@ -413,11 +436,10 @@
         )
 
     note[7:8, 2 * B :] = jnp.zeros((1, 2 * B), F32)
-    t = jnp.concatenate([in_vec[r, pl.ds(b, 1), :] for r in runs], axis=0)
     ts, ys = [t], []
     basis[4] = t
     for turn in range(4):
-        ys.append(solve(ts[turn]))
+        ys.append(solve(begin(ts[turn]) if turn else begun))
         basis[turn] = ys[turn]
         if turn == 3:
             break

time: 58 us -> 56 us (0.966)
  Pallas kernels: 55.9 us -> 53.9 us
    pallas_call x1, Pallas kernels: 55.9 us -> 53.9 us  [local(): pl.pallas_call(functools.partial(kernel, (nl, ns, ny)), out_shape=shape((...]
where the time goes in v5:
time: 56 us; the launch traced here: 55.9 us
  Pallas kernels  53.9 us (96%)
  local copies, waits for them, and re-layouts  1.33 us (2%)
  between operations  0.64 us (1%)
    pallas_call x1, Pallas kernels, local(): pl.pallas_call(functools.partial(kernel, (nl, ns, ny)), out_shape=shape((...  53.9 us
    slice x1, local copies, waits for them, and re-layouts, local(): return (out[:2], out[2:])  1.33 us

profile of v5, /device:TPU:1, one launch (start us, length us, event | category | flops | bytes accessed | tf_op | source)
XLA Modules:
  0.0 55.9 jit_solution(18132983566348299074)
XLA Ops:
  0.6 53.9 %line_cg.1 = f32[4,256]{1,0:T(4,128)} custom-call(f32[2,4,4096]{2,1,0:T(4,128)} %diag_in.1, f32[2,4,4096]{2,1,0:T(4,128)} %coup_in.1, f32[2,256]{1,0:T(2,128)} %weight_in.1, f32[2,256]{1,0:T(2,128)} %right_in.1), custom_call_target="tpu_custom_call" | custom-call | tf_op jit(solution)/shard_map/line_cg/pallas_call | solution.py:571
  54.5 1.3 %fusion = (f32[2,256]{1,0:T(2,128)}, f32[2,256]{1,0:T(2,128)}) fusion(f32[4,256]{1,0:T(4,128)} %line_cg.1), kind=kLoop, calls=%fused_computation | loop fusion | bytes 8192 | tf_op jit(solution)/shard_map/slice | solution.py:631

commit v6 on v5

--- a/solution.py
+++ b/solution.py
@@ -55,60 +55,80 @@
     return jnp.broadcast_to(x[j : j + 1], x.shape)
 
 
-def invert(work, packs, beside=iter(())):
+def invert(work, packs, beside=iter(()), tiles=1):
     shape = (8, 2 * B)
+    wide = 8 * tiles
+    size = work.shape[1]
+    paired = size == B
     sub, lane = iota(shape, 0), iota(shape, 1)
     low = lane < B
-    half = jnp.where(low, 0, B)
-    lane_all = iota((B, 2 * B), 1)
-    half_all = jnp.where(lane_all < B, 0, B)
+    lane_all = iota((size, 2 * B), 1)
+    half = jnp.where(low, 0, B) if paired else jnp.zeros_like(lane)
+    half_all = jnp.where(lane_all < B, 0, B) if paired else jnp.zeros_like(lane_all)
     none = jnp.zeros(shape, F32)
-    every = range(packs)
+    every, each = range(packs), range(tiles)
 
     def gather(x, at):
         return [jnp.take_along_axis(x, i, axis=1, mode="promise_in_bounds") for i in at]
 
-    def less(x, x_cols, new, inside):
-        c = [x_cols[j] * row_of(new, j) for j in range(8)]
-        total = ((c[0] + c[1]) + (c[2] + c[3])) + ((c[4] + c[5]) + (c[6] + c[7]))
-        return jnp.where(inside, 0.0, x) - total
+    def total(terms):
+        while len(terms) > 1:
+            terms = [x + y for x, y in zip(terms[::2], terms[1::2])]
+        return terms[0]
+
+    def cut(x, base):
+        return [x[base + 8 * t : base + 8 * t + 8] for t in each]
 
     whole = [work[p] for p in every]
-    rows = [x[:8] for x in whole]
-    for q in range(B // 8):
-        next(beside, None)
-        base = 8 * q
+    rows = [cut(x, 0) for x in whole]
+    for q in range(size // wide):
+        for _ in each:
+            next(beside, None)
+        base = wide * q
         within = lane - half - base
-        inside = jnp.logical_and(within >= 0, within < 8)
+        inside = jnp.logical_and(within >= 0, within < wide)
         within_all = lane_all - half_all - base
-        inside_all = jnp.logical_and(within_all >= 0, within_all < 8)
-        at = [half + base + j for j in range(8)]
-        cols = [gather(r, at) for r in rows]
-        more = q + 1 < B // 8
+        inside_all = jnp.logical_and(within_all >= 0, within_all < wide)
+        at = [half + base + j for j in range(wide)]
+        cols = [[gather(x, at) for x in r] for r in rows]
+        more = base + wide < size
         if more:
-            after = [x[base + 8 : base + 16] for x in whole]
-            after_cols = [gather(x, at) for x in after]
-        rows = [jnp.where(inside, jnp.where(within == sub, 1.0, 0.0), r) for r in rows]
-        scale = [none for _ in every]
-        for j in range(8):
-            mine = sub == j
+            after = [cut(x, base + wide) for x in whole]
+            after_cols = [[gather(x, at) for x in r] for r in after]
+        rows = [[jnp.where(inside, jnp.where(within == sub + 8 * t, 1.0, 0.0), r[t]) for t in each] for r in rows]
+        scale = [[none for _ in each] for _ in every]
+        for j in range(wide):
+            own, at_row = j // 8, j % 8
+            mine = sub == at_row
             for p in every:
                 g = cols[p]
-                inverse = 1.0 / row_of(g[j], j)
-                ratio = jnp.where(mine, 0.0, g[j]) * inverse
-                scale[p] = jnp.where(mine, inverse, scale[p])
-                for c in range(j + 1, 8):
-                    g[c] = g[c] - ratio * row_of(g[c], j)
-                rows[p] = rows[p] - ratio * row_of(rows[p], j)
+                inverse = 1.0 / row_of(g[own][j], at_row)
+                ratio = [(jnp.where(mine, 0.0, g[t][j]) if t == own else g[t][j]) * inverse for t in each]
+                scale[p][own] = jnp.where(mine, inverse, scale[p][own])
+                for c in range(j + 1, wide):
+                    pivot = row_of(g[own][c], at_row)
+                    for t in each:
+                        g[t][c] = g[t][c] - ratio[t] * pivot
+                pivot = row_of(rows[p][own], at_row)
+                rows[p] = [rows[p][t] - ratio[t] * pivot for t in each]
         for p in every:
-            new = rows[p] * scale[p]
-            left, right = jnp.where(low, new, 0.0), jnp.where(low, 0.0, new)
-            weights = jnp.concatenate([none] * q + [left] + [none] * 7 + [right] + [none] * (7 - q), axis=0)
+            new = [rows[p][t] * scale[p][t] for t in each]
+            before, behind = [none] * (base // 8), [none] * ((size - base) // 8 - tiles)
+            placed = before + new + behind
+            if paired:
+                left = before + [jnp.where(low, x, 0.0) for x in new] + behind
+                placed = left + before + [jnp.where(low, 0.0, x) for x in new] + behind
+            weights = jnp.concatenate(placed, axis=0)
             rest = jnp.where(inside_all, 0.0, whole[p]) - mm(jnp.where(inside_all, whole[p], 0.0), weights)
-            parts = ([rest[:base]] if q else []) + [new] + ([rest[base + 8 :]] if more else [])
+            parts = ([rest[:base]] if q else []) + new + ([rest[base + wide :]] if more else [])
             whole[p] = jnp.concatenate(parts, axis=0)
             if more:
-                rows[p] = less(after[p], after_cols[p], new, inside)
+                spread_rows = [row_of(new[j // 8], j % 8) for j in range(wide)]
+                rows[p] = [
+                    jnp.where(inside, 0.0, after[p][t])
+                    - total([x * y for x, y in zip(after_cols[p][t], spread_rows)])
+                    for t in each
+                ]
     for p in every:
         work[p] = whole[p]
 
@@ -129,7 +149,7 @@
 
 def kernel(
     dims, diag_in, coup_in, weight_in, right_in, out, diag, coup, weight, right, in_sem,
-    dch, pch, vec, in_d13, in_p10, in_d20, in_p23, in_vec, work, uq_s, et_s, xy_s,
+    dch, pch, vec, in_d13, in_p10, in_d20, in_p23, in_vec, work, middle, uq_s, et_s, xy_s,
     w1h, w1l, w2h, w2l, w3h, w3l, basis, edge_in, wbuf, wline, plane_w, note, notes, ahead, mine, theirs, sums, sums_in,
     gat_send, gat_recv, edge_send, edge_recv, pw_send, pw_recv, note_send, note_recv, ahead_send, ahead_recv,
     part_sem, sum_send, sum_recv,
@@ -384,23 +404,17 @@
 
     s0, s1, s2, s3 = (separator(r) for r in runs)
     work[0] = jnp.concatenate([s0, s3], axis=1)
-    invert(work, 1, beside)
+    invert(work, 1, beside, 2)
     j0, j3 = work[0, :, :B], work[0, :, B:]
     v0, v3 = mm(j0, zs[0]), mm(j3, zts[2])
     s1 = s1 - mm(zts[0], v0)
     s2 = s2 - mm(zs[2], v3)
-    work[0] = jnp.concatenate([s1, s2], axis=1)
-    invert(work, 1, beside)
-    v12, v21 = mm(work[0, :, :B], zs[1]), mm(work[0, :, B:], zts[1])
-    work[0] = jnp.concatenate([s1 - mm(zs[1], v21), s2 - mm(zts[1], v12)], axis=1)
-    invert(work, 1, beside)
+    middle[0, :B, :] = jnp.concatenate([s1, -zs[1]], axis=1)
+    middle[0, B:, :] = jnp.concatenate([-zts[1], s2], axis=1)
+    invert(middle, 1, beside, 2)
     for _ in beside:
         pass
-    e11, e22 = work[0, :, :B], work[0, :, B:]
-    e12, e21 = mm(v12, e22), mm(v21, e11)
-    inner = jnp.concatenate(
-        [jnp.concatenate([e11, e12], axis=1), jnp.concatenate([e21, e22], axis=1)], axis=0
-    )
+    inner = middle[0]
     zero = jnp.zeros((B, B), F32)
     v = jnp.concatenate([jnp.concatenate([v0, zero], axis=1), jnp.concatenate([zero, v3], axis=1)], axis=0)
     side = mm(v, inner)
@@ -588,6 +602,7 @@
             vmem((ns, B, 2 * B), F32),
             vmem((ns, 4, 4 * B), F32),
             vmem((ns // 2, B, 2 * B), F32),
+            vmem((1, 2 * B, 2 * B), F32),
             vmem((ns, 2 * B, 2 * B), F32),
             vmem((ns, B, 2 * B), F32),
             vmem((ns, B, 2 * B), F32),

time: 56 us -> 54.2 us (0.968)
  Pallas kernels: 53.9 us -> 52.1 us
    pallas_call x1, Pallas kernels: 53.9 us -> 52.1 us  [local(): pl.pallas_call(functools.partial(kernel, (nl, ns, ny)), out_shape=shape((...]
where the time goes in v6:
time: 54.2 us; the launch traced here: 54 us
  Pallas kernels  52.1 us (96%)
  local copies, waits for them, and re-layouts  1.33 us (2%)
  between operations  0.64 us (1%)
    pallas_call x1, Pallas kernels, local(): pl.pallas_call(functools.partial(kernel, (nl, ns, ny)), out_shape=shape((...  52.1 us
    slice x1, local copies, waits for them, and re-layouts, local(): return (out[:2], out[2:])  1.33 us

profile of v6, /device:TPU:1, one launch (start us, length us, event | category | flops | bytes accessed | tf_op | source)
XLA Modules:
  0.0 54.0 jit_solution(11577575993478614248)
XLA Ops:
  0.6 52.1 %line_cg.1 = f32[4,256]{1,0:T(4,128)} custom-call(f32[2,4,4096]{2,1,0:T(4,128)} %diag_in.1, f32[2,4,4096]{2,1,0:T(4,128)} %coup_in.1, f32[2,256]{1,0:T(2,128)} %weight_in.1, f32[2,256]{1,0:T(2,128)} %right_in.1), custom_call_target="tpu_custom_call" | custom-call | tf_op jit(solution)/shard_map/line_cg/pallas_call | solution.py:585
  52.7 1.3 %fusion = (f32[2,256]{1,0:T(2,128)}, f32[2,256]{1,0:T(2,128)}) fusion(f32[4,256]{1,0:T(4,128)} %line_cg.1), kind=kLoop, calls=%fused_computation | loop fusion | bytes 8192 | tf_op jit(solution)/shard_map/slice | solution.py:646

commit v7 on v6

--- a/solution.py
+++ b/solution.py
@@ -143,18 +143,21 @@
     wide = jnp.broadcast_to(row, (16, row.shape[1]))
     high = wide.astype(BF16).astype(F32)
     both = jnp.where(iota(wide.shape, 0) == 0, high, wide - high).astype(BF16)
-    out = sum(jnp.dot(both, w, preferred_element_type=F32) for w in weights)
+    out = jnp.dot(jnp.concatenate([both, both], axis=1), weights, preferred_element_type=F32)
     return out[:1] + out[1:2]
 
 
 def kernel(
     dims, diag_in, coup_in, weight_in, right_in, out, diag, coup, weight, right, in_sem,
     dch, pch, vec, in_d13, in_p10, in_d20, in_p23, in_vec, work, middle, uq_s, et_s, xy_s,
-    w1h, w1l, w2h, w2l, w3h, w3l, basis, edge_in, wbuf, wline, plane_w, note, notes, ahead, mine, theirs, sums, sums_in,
+    w1, w2, w3, basis, edge_in, wbuf, wline, plane_w, note, notes, ahead, mine, theirs, sums, sums_in,
     gat_send, gat_recv, edge_send, edge_recv, pw_send, pw_recv, note_send, note_recv, ahead_send, ahead_recv,
     part_sem, sum_send, sum_recv,
 ):
     nl, ns, ny = dims
+    w1h, w1l = w1.at[:, : 4 * B, :], w1.at[:, 4 * B :, :]
+    w2h, w2l = w2.at[: 8 * B, :], w2.at[8 * B :, :]
+    w3h, w3l = w3.at[:, : 4 * B, :], w3.at[:, 4 * B :, :]
     m, s = lax.axis_index("lines"), lax.axis_index("seg")
     core, y_at, z_at = lax.rem(m, 2), lax.rem(m // 2, ny), m // (2 * ny)
     nz = nl // (2 * ny)
@@ -186,7 +189,8 @@
     sends_across = rank == 0
     peers = [(m, x) for x in others]
     for place, size, own in groups[::-1]:
-        peers += [place(lax.rem(own + d, size)) for d in range(1, size)]
+        away = sorted(range(1, size), key=lambda d: -min(d, size - d))
+        peers += [place(lax.rem(own + d, size)) for d in away]
     peers += [other, herald]
     pairs = ((diag_in, diag), (coup_in, coup), (weight_in, weight), (right_in, right))
     loads = [pltpu.make_async_copy(src, dst, in_sem.at[i]) for i, (src, dst) in enumerate(pairs)]
@@ -226,6 +230,13 @@
     pl.semaphore_wait(barrier, len(peers) + jnp.where(sends_across, many, 0))
 
     sends = []
+
+    def drain(keep):
+        gone = sends[: len(sends) - keep]
+        del sends[: len(gone)]
+        for copy in gone:
+            copy.wait_send()
+
     chunks = ((dch, 1, in_d13), (pch, 1, in_p10), (dch, 2, in_d20), (pch, 2, in_p23))
 
     def chunk_copy(i, to, slot, d):
@@ -290,7 +301,7 @@
         return finish
 
     def spread(place, size, own, source, inbox, send_sem, recv_sem):
-        for d in range(1, size):
+        for d in sorted(range(1, size), key=lambda d: -min(d, size - d)):
             copy = pltpu.make_async_remote_copy(
                 src_ref=source,
                 dst_ref=inbox.at[own],
@@ -346,7 +357,7 @@
     w_own = jnp.concatenate([in_vec[r, pl.ds(3, 1), :] for r in runs], axis=0)
     wbuf[...] = w_own
     wait_weights = exchange(4, wbuf, ((1, other),))
-    invert(work, ns // 2)
+    invert(work, ns // 2, tiles=2)
     zs, zts, ss, fts, i2s = [], [], [], [], []
     eye = jnp.where(iota((B, 2 * B), 0) + B == iota((B, 2 * B), 1), 1.0, 0.0)
     for r in runs:
@@ -393,7 +404,7 @@
             if r < ns - 1:
                 store_split(w3h, w3l, (r, slice(B * r + B, B * r + 2 * B)), ht[:B])
             yield
-            begun.append(apply(t[r : r + 1], (w1h[r], w1l[r])))
+            begun.append(apply(t[r : r + 1], w1[r]))
             yield
 
     beside = operators()
@@ -432,12 +443,12 @@
         store_split(w2h, w2l, (slice(2 * B * r + B, 2 * B * r + 2 * B),), rows[r])
 
     def begin(t):
-        return [apply(t[r : r + 1], (w1h[r], w1l[r])) for r in runs]
+        return [apply(t[r : r + 1], w1[r]) for r in runs]
 
     def solve(first):
         f = jnp.concatenate([x[:, 4 * B :] for x in first], axis=1)
-        u = apply(f, (w2h[...], w2l[...]))
-        out = [first[r][:, : 4 * B] + apply(u, (w3h[r], w3l[r])) for r in runs]
+        u = apply(f, w2[...])
+        out = [first[r][:, : 4 * B] + apply(u, w3[r]) for r in runs]
         return jnp.concatenate(out, axis=0)
 
     def folded(x):
@@ -458,6 +469,7 @@
         if turn == 3:
             break
         arrive = exchange(turn, basis.at[turn], ((0, partner), (1, other)))
+        drain(2)
         if turn == 0:
             wline[...] = jnp.where(b == 0, w_mate, w_own)
             wait_plane = spread(near, many, rank, wline, plane_w, pw_send, pw_recv)
@@ -473,8 +485,6 @@
     note[0:4, :] = ys[3]
     moment(5)
     moment(6)
-    wait_notes = spread(near, many, rank, note, notes, note_send, note_recv)
-
     def across(to):
         return pltpu.make_async_remote_copy(
             src_ref=note.at[...],
@@ -487,10 +497,12 @@
 
     @pl.when(sends_across)
     def _():
-        for i in range(many):
+        for i in sorted(range(many), key=lambda i: -min(i, many - i)):
             across(i).start()
 
+    wait_notes = spread(near, many, rank, note, notes, note_send, note_recv)
     arrive = exchange(3, basis.at[3], ((0, partner), (1, other)))
+    drain(many + 1)
     wait_plane()
     wait_notes()
     pltpu.make_async_remote_copy(
@@ -525,6 +537,13 @@
         device_id_type=MESH,
     )
     swap_copy.start()
+    drain(nz - 1)
+
+    @pl.when(sends_across)
+    def _():
+        for i in range(many):
+            across(i).wait_send()
+
     wait_sums()
     total = sums_in[0]
     for i in range(1, nz):
@@ -566,13 +585,7 @@
     out[pl.ds(1, 1), :] = jnp.where(first, x_theirs, x_mine)
     out[pl.ds(2, 1), :] = jnp.where(first, r_mine, r_theirs)
     out[pl.ds(3, 1), :] = jnp.where(first, r_theirs, r_mine)
-    for copy in sends:
-        copy.wait_send()
-
-    @pl.when(sends_across)
-    def _():
-        for i in range(many):
-            across(i).wait_send()
+    drain(0)
 
 
 def local(diag_blocks, couplings, cross_weight, right_side):
@@ -606,12 +619,9 @@
             vmem((ns, 2 * B, 2 * B), F32),
             vmem((ns, B, 2 * B), F32),
             vmem((ns, B, 2 * B), F32),
-            vmem((ns, 4 * B, 6 * B), BF16),
-            vmem((ns, 4 * B, 6 * B), BF16),
-            vmem((8 * B, 4 * B), BF16),
-            vmem((8 * B, 4 * B), BF16),
-            vmem((ns, 4 * B, 4 * B), BF16),
-            vmem((ns, 4 * B, 4 * B), BF16),
+            vmem((ns, 8 * B, 6 * B), BF16),
+            vmem((16 * B, 4 * B), BF16),
+            vmem((ns, 8 * B, 4 * B), BF16),
             vmem((9, 4, 4 * B), F32),
             vmem((5, 2, 4, 4 * B), F32),
             vmem((4, 4 * B), F32),

time: 54.2 us -> 53.9 us (level)
  no operation moved by 1% of the time
where the time goes in v7:
time: 53.9 us; the launch traced here: 53.8 us
  Pallas kernels  51.8 us (96%)
  local copies, waits for them, and re-layouts  1.33 us (2%)
  between operations  0.64 us (1%)
    pallas_call x1, Pallas kernels, local(): pl.pallas_call(functools.partial(kernel, (nl, ns, ny)), out_shape=shape((...  51.8 us
    slice x1, local copies, waits for them, and re-layouts, local(): return (out[:2], out[2:])  1.33 us

profile of v7, /device:TPU:1, one launch (start us, length us, event | category | flops | bytes accessed | tf_op | source)
XLA Modules:
  0.0 53.8 jit_solution(5059606144974630102)
XLA Ops:
  0.6 51.8 %line_cg.1 = f32[4,256]{1,0:T(4,128)} custom-call(f32[2,4,4096]{2,1,0:T(4,128)} %diag_in.1, f32[2,4,4096]{2,1,0:T(4,128)} %coup_in.1, f32[2,256]{1,0:T(2,128)} %weight_in.1, f32[2,256]{1,0:T(2,128)} %right_in.1), custom_call_target="tpu_custom_call" | custom-call | tf_op jit(solution)/shard_map/line_cg/pallas_call | solution.py:598
  52.4 1.3 %fusion = (f32[2,256]{1,0:T(2,128)}, f32[2,256]{1,0:T(2,128)}) fusion(f32[4,256]{1,0:T(4,128)} %line_cg.1), kind=kLoop, calls=%fused_computation | loop fusion | bytes 8192 | tf_op jit(solution)/shard_map/slice | solution.py:656
